TPU v7x, 32 devices: a whole 2x2x4 slice. The times are simulated.
32 devices in a mesh: row: 4 (over y, x), col: 8 (over z, core).
Axes of the slice: x: 2, y: 2, z: 4, core: 2. Of those that a mesh axis runs over, the one named last changes fastest.
Arguments:
- pair_tensor: bfloat16 [1024, 1024, 128], P('row', 'col'), may hold values from -6 to 6
- token_single: bfloat16 [1024, 768], P('row'), may hold values from -6 to 6
- atom_single: bfloat16 [8192, 128], P(('row', 'col')), may hold values from -6 to 6
- atom_token: int32 [8192], replicated, may hold values from 0 to 1023, as said below
- chain_index: int32 [1024], replicated, may hold values from 0 to 15, never falling along the last dimension, each value on 1 to 256 neighbouring positions
- pair_up: bfloat16 [128, 512], replicated, may hold values from -0.5 to 0.5
- pair_down: bfloat16 [256, 128], replicated, may hold values from -0.75 to 0.75
- bias_heads: bfloat16 [128, 20], replicated, may hold values from -0.5 to 0.5
- atom_gain: float32 [128], replicated, may hold values from 0.1 to 1.9
- atom_proj: bfloat16 [128, 512], replicated, may hold values from -0.5 to 0.5
- atom_exit: bfloat16 [128, 128], replicated, may hold values from -0.5 to 0.5
- atom_pool: bfloat16 [128, 768], replicated, may hold values from -0.5 to 0.5
- token_gain: float32 [768], replicated, may hold values from 0.1 to 1.9
- token_proj: bfloat16 [768, 3072], replicated, may hold values from -0.21875 to 0.21875
- token_exit: bfloat16 [768, 768], replicated, may hold values from -0.21875 to 0.21875
- chain_bias: float32 [16], replicated, may hold values from -2 to 115
- token_back: bfloat16 [768, 128], replicated, may hold values from -0.21875 to 0.21875
Outputs:
- token_update: bfloat16 [1024, 768], P('row')
- atom_update: bfloat16 [8192, 128], P(('row', 'col'))
Inputs may be any that keep to these rules, and one draw needn't show every extreme that they name: `atom_token`: Non-decreasing. For every r, the atoms r * 8 * 256 to (r + 1) * 8 * 256 - 1 belong to the tokens r * 256 to (r + 1) * 256 - 1, and every token has one atom or more.
All inputs are finite; a program needn't handle non-finite values.
Results may differ from a plain program's by a relative error of at most 0.0085.
Values may be sent and summed in bfloat16 or wider, within the bound.
A program may use at most 128 MiB of HBM per device.

v0:
```python
import jax
import jax.numpy as jnp
from jax import lax
from jax.sharding import PartitionSpec as P

CZ = 128
CS = 768
CA = 128
HT = 16
HA = 4
PH = 256
QB = 32
KW = 128
EDGE = 48
HDA = 32
HDT = 48
HB = 20


EPS = 1e-05


def with_halo(cells, sides, width):
    for axis, dim in sides:
        count = lax.axis_size(axis)
        ends = count - 1
        head = lax.slice_in_dim(cells, 0, width, axis=dim)
        tail = lax.slice_in_dim(cells, cells.shape[dim] - width, cells.shape[dim], axis=dim)
        cells = jnp.concatenate(
            [
                lax.ppermute(tail, axis, [(i, (i + 1) % count) for i in range(ends)]),
                cells,
                lax.ppermute(head, axis, [((i + 1) % count, i) for i in range(ends)]),
            ],
            axis=dim,
        )
    return cells


def joined(value, axis, join):
    pieces = jax.tree.map(lambda part: lax.all_gather(part, axis), value)
    head = jax.tree.map(lambda part: part[0], pieces)
    tail = jax.tree.map(lambda part: part[1:], pieces)
    total, _ = lax.scan(lambda total, piece: (join(total, piece), None), head, tail)
    return total


def standardize(features):
    features = features.astype(jnp.float32)
    center = features - jnp.mean(features, axis=-1, keepdims=True)
    spread = jnp.mean(center * center, axis=-1, keepdims=True)
    return center * lax.rsqrt(spread + EPS)


def normalize(features, gain_vec):
    return standardize(features) * gain_vec


def merge_parts(earlier, later):
    top_early, sum_early, out_early = earlier
    top_late, sum_late, out_late = later
    row_top = jnp.maximum(top_early, top_late)
    scale_early = jnp.exp(top_early - row_top)
    scale_late = jnp.exp(top_late - row_top)
    head_width = out_early.shape[1] // top_early.shape[0]
    merged_out = out_early * jnp.repeat(scale_early.T, head_width, axis=1) + out_late * jnp.repeat(
        scale_late.T, head_width, axis=1
    )
    return (row_top, sum_early * scale_early + sum_late * scale_late, merged_out)


def local(
    pair_tensor,
    token_single,
    atom_single,
    atom_token,
    chain_index,
    pair_up,
    pair_down,
    bias_heads,
    atom_gain,
    atom_proj,
    atom_exit,
    atom_pool,
    token_gain,
    token_proj,
    token_exit,
    chain_bias,
    token_back,
):
    tok_rows = token_single.shape[0]
    tok_cols = pair_tensor.shape[1]
    atom_rows = atom_single.shape[0]
    row_count = lax.axis_size("row")
    col_count = lax.axis_size("col")
    row_index = lax.axis_index("row")
    col_index = lax.axis_index("col")
    row_start = row_index * tok_rows
    rows_per = tok_rows // 16
    pair_blocks = pair_tensor.reshape(16, rows_per * tok_cols, CZ)

    def pair_step(pair_part):
        normed = standardize(pair_part).astype(jnp.bfloat16)
        mixed_up = jnp.dot(normed, pair_up, preferred_element_type=jnp.float32)
        hidden = (jax.nn.silu(mixed_up[:, :PH]) * mixed_up[:, PH:]).astype(jnp.bfloat16)
        updated = pair_part.astype(jnp.float32) + jnp.dot(
            hidden, pair_down, preferred_element_type=jnp.float32
        )
        normed_two = standardize(updated).astype(jnp.bfloat16)
        return jnp.einsum(
            "nc,ch->hn", normed_two, bias_heads, preferred_element_type=jnp.float32
        ).astype(jnp.bfloat16)

    biases = lax.map(pair_step, pair_blocks).reshape(16, HB, rows_per, tok_cols)
    biases = jnp.transpose(biases, (1, 0, 2, 3)).reshape(HB, tok_rows, tok_cols)
    atom_bias = biases[:HA]
    token_bias = biases[HA:]
    band_bias = lax.all_gather(atom_bias, "col", axis=2, tiled=True)
    atom_normed = normalize(atom_single, atom_gain).astype(jnp.bfloat16)
    atom_projected = jnp.dot(atom_normed, atom_proj, preferred_element_type=jnp.float32)
    queries = atom_projected[:, :CA].astype(jnp.bfloat16)
    keyvals = atom_projected[:, CA : 3 * CA].astype(jnp.bfloat16)
    atom_gate = atom_projected[:, 3 * CA :]
    extended = with_halo(keyvals, ((("row", "col"), 0),), EDGE)
    nblocks = atom_rows // QB
    windows = jnp.stack(
        [
            lax.slice_in_dim(extended, QB * block_id, QB * block_id + KW, axis=0)
            for block_id in range(nblocks)
        ]
    )
    total_atoms = atom_rows * col_count * row_count
    atom_base = (row_index * col_count + col_index) * atom_rows
    positions = (
        atom_base
        + QB * jnp.arange(nblocks, dtype=jnp.int32)[:, None]
        - EDGE
        + jnp.arange(KW, dtype=jnp.int32)[None, :]
    )
    in_range = (positions >= 0) & (positions < total_atoms)
    key_tokens = atom_token[jnp.clip(positions, 0, total_atoms - 1)]
    query_tokens = lax.dynamic_slice_in_dim(atom_token, atom_base, atom_rows).reshape(nblocks, QB)
    q_first = jnp.clip(query_tokens[:, 0] - row_start, 0, band_bias.shape[1] - QB)
    k_first = jnp.clip(key_tokens[:, 0], 0, band_bias.shape[2] - KW)

    def tile_at(q_at, k_at):
        return lax.dynamic_slice(band_bias, (jnp.int32(0), q_at, k_at), (HA, QB, KW))

    tile_stack = jax.vmap(tile_at)(q_first, k_first)
    q_onehot = (
        (query_tokens - row_start - q_first[:, None])[:, :, None]
        == jnp.arange(QB, dtype=jnp.int32)[None, None, :]
    ).astype(jnp.bfloat16)
    k_onehot = (
        (key_tokens - k_first[:, None])[:, :, None]
        == jnp.arange(KW, dtype=jnp.int32)[None, None, :]
    ).astype(jnp.bfloat16)
    rows_sel = jnp.einsum(
        "bia,bhac->bhic", q_onehot, tile_stack, preferred_element_type=jnp.float32
    ).astype(jnp.bfloat16)
    bias_tile = jnp.einsum("bhic,bjc->bhij", rows_sel, k_onehot, preferred_element_type=jnp.float32)
    query_heads = queries.reshape(nblocks, QB, HA, CA // HA)
    keys_win = windows[:, :, :CA].reshape(nblocks, KW, HA, CA // HA)
    vals_win = windows[:, :, CA:].reshape(nblocks, KW, HA, CA // HA)
    scores = (
        jnp.einsum("bihd,bjhd->bhij", query_heads, keys_win, preferred_element_type=jnp.float32)
        * HDA ** (-0.5)
        + bias_tile
    )
    scores = jnp.where(in_range[:, None, None, :], scores, -1e30)
    row_top = jnp.max(scores, axis=-1, keepdims=True)
    weights_full = jnp.exp(scores - row_top)
    denominator = jnp.sum(weights_full, axis=-1)
    attended = jnp.einsum(
        "bhij,bjhd->bihd",
        weights_full.astype(jnp.bfloat16),
        vals_win,
        preferred_element_type=jnp.float32,
    )
    attended = (attended / jnp.transpose(denominator, (0, 2, 1))[..., None]).reshape(atom_rows, CA)
    atom_gated = (attended * jax.nn.sigmoid(atom_gate)).astype(jnp.bfloat16)
    atom_mid = (
        atom_single.astype(jnp.float32)
        + jnp.dot(atom_gated, atom_exit, preferred_element_type=jnp.float32)
    ).astype(jnp.bfloat16)
    atom_pooled = jax.nn.relu(
        jnp.dot(atom_mid, atom_pool, preferred_element_type=jnp.float32)
    ).astype(jnp.bfloat16)
    local_tok = query_tokens.reshape(atom_rows) - row_start
    onehot = (local_tok[:, None] == jnp.arange(tok_rows, dtype=jnp.int32)[None, :]).astype(
        jnp.bfloat16
    )
    partial_value = jnp.einsum("at,ac->tc", onehot, atom_pooled, preferred_element_type=jnp.float32)
    row_atoms = lax.dynamic_slice_in_dim(
        atom_token, row_index * atom_rows * col_count, atom_rows * col_count
    )
    counts = jnp.sum(
        (row_atoms[None, :] - row_start == jnp.arange(tok_rows, dtype=jnp.int32)[:, None]).astype(
            jnp.float32
        ),
        axis=1,
    )
    summed = lax.psum(partial_value, "col")
    token_mid = (token_single.astype(jnp.float32) + summed / counts[:, None]).astype(jnp.bfloat16)
    token_normed = normalize(token_mid, token_gain).astype(jnp.bfloat16)
    row_proj = jnp.dot(token_normed, token_proj[:, : 2 * CS], preferred_element_type=jnp.float32)
    row_query = row_proj[:, :CS].astype(jnp.bfloat16)
    token_gate = row_proj[:, CS:]
    every_token = lax.all_gather(token_normed, "row", axis=0, tiled=True)
    col_tokens = lax.dynamic_slice_in_dim(every_token, col_index * tok_cols, tok_cols)
    col_proj = jnp.dot(
        col_tokens, token_proj[:, 2 * CS :], preferred_element_type=jnp.float32
    ).astype(jnp.bfloat16)
    col_keys = col_proj[:, :CS].reshape(tok_cols, HT, HDT)
    col_values = col_proj[:, CS:].reshape(tok_cols, HT, HDT)
    row_chain = lax.dynamic_slice_in_dim(chain_index, row_start, tok_rows)
    col_chain = lax.dynamic_slice_in_dim(chain_index, col_index * tok_cols, tok_cols)
    same_chain = (row_chain[:, None] == col_chain[None, :]).astype(jnp.float32)
    token_scores = (
        jnp.einsum(
            "ihd,jhd->hij",
            row_query.reshape(tok_rows, HT, HDT),
            col_keys,
            preferred_element_type=jnp.float32,
        )
        * HDT ** (-0.5)
        + token_bias.astype(jnp.float32)
        + chain_bias[:, None, None] * same_chain[None]
    )
    local_top = jnp.max(token_scores, axis=-1)
    local_exp = jnp.exp(token_scores - local_top[:, :, None])
    local_sum = jnp.sum(local_exp, axis=-1)
    local_out = jnp.einsum(
        "hij,jhd->ihd",
        local_exp.astype(jnp.bfloat16),
        col_values,
        preferred_element_type=jnp.float32,
    ).reshape(tok_rows, CS)
    merged_top, merged_sum, merged_out = joined(
        (local_top, local_sum, local_out), "col", merge_parts
    )
    token_attended = merged_out / jnp.repeat(merged_sum.T, HDT, axis=1)
    token_gated = (token_attended * jax.nn.sigmoid(token_gate)).astype(jnp.bfloat16)
    token_update = (
        token_mid.astype(jnp.float32)
        + jnp.dot(token_gated, token_exit, preferred_element_type=jnp.float32)
    ).astype(jnp.bfloat16)
    token_sent = jnp.dot(token_update, token_back, preferred_element_type=jnp.float32).astype(
        jnp.bfloat16
    )
    atom_added = jnp.dot(onehot, token_sent, preferred_element_type=jnp.float32)
    atom_update = (atom_mid.astype(jnp.float32) + atom_added).astype(jnp.bfloat16)
    return (token_update, atom_update)


def solution(mesh):
    placed = (
        P("row", "col", None),
        P("row", None),
        P(("row", "col"), None),
        P(),
        P(),
        P(),
        P(),
        P(),
        P(),
        P(),
        P(),
        P(),
        P(),
        P(),
        P(),
        P(),
        P(),
    )
    return jax.shard_map(
        local,
        mesh=mesh,
        in_specs=placed,
        out_specs=(P("row", None), P(("row", "col"), None)),
        check_vma=False,
    )
```

profile of v0, /device:TPU:0, one launch (start us, length us, event | category | flops | bytes accessed | tf_op | source)
XLA Modules:
  0.0 371.2 jit_solution(14095179366481358769)
XLA Ops:
  7.2 69.6 %while.25 = (s32[]{:T(128)}, bf16[16,20,2048]{2,1,0:T(8,128)(2,1)}, bf16[16,2048,128]{2,1,0:T(8,128)(2,1)}, bf16[128,512]{1,0:T(8,128)(2,1)}, bf16[256,128]{1,0:...) while((s32[]{:T(128)}, bf16[16,20,2048]{2,1,0:T(8,128)(2,1)}, bf16[16,2048,128]{2,1,0:T(8,128)(2,1)}, ...), condition=%wide.region_7.8_spmd, body=%wide.region_2.7_spmd.sunk | while | flops 421310464 | bytes 16983216 | solution.py:114
  7.3 1.2 constant_dynamic-slice_fusion.6
  11.7 1.1 constant_dynamic-slice_fusion.6
  16.0 1.1 constant_dynamic-slice_fusion.6
  20.4 1.1 constant_dynamic-slice_fusion.6
  29.1 1.1 constant_dynamic-slice_fusion.6
  33.4 1.1 constant_dynamic-slice_fusion.6
  42.1 1.1 constant_dynamic-slice_fusion.6
  50.8 1.1 constant_dynamic-slice_fusion.6
  76.8 3.5 reshape.301
  80.3 1.7 copy.109
  84.3 1.3 collective-permute-start.1
  85.6 3.0 collective-permute-start
  88.9 6.1 %gather_fusion = s32[1024]{0:T(1024)S(1)} fusion(s32[8192]{0:T(1024)S(1)} %copy-done.1, s32[1024]{0:T(1024)S(1)} %fusion.93), kind=kCustom, calls=%fused_computation | custom fusion | bytes 12288 | tf_op jit(solution)/shard_map/gather | solution.py:141
  97.7 1.2 convolution_multiply_fusion
  98.8 17.9 %all-gather.6.cloned.1.call-done = bf16[4,256,1024]{2,1,0:T(8,128)(2,1)} async-done(((bf16[4,256,128]{2,1,0:T(8,128)(2,1)}), bf16[4,256,1024]{2,1,0:T(8,128)(2,1)}) %all-gather.6.cloned.1.call-update) | async-done | bytes 2097168 | tf_op jit(solution)/shard_map/all_gather | solution.py:118
  116.8 27.5 %while.27 = (s32[]{:T(128)}, bf16[4,256,1024]{2,1,0:T(8,128)(2,1)}, s32[8,3]{1,0:T(8,128)S(1)}, bf16[8,4,32,128]{3,2,1,0:T(8,128)(2,1)}, s32[]{:T(128)}) while((s32[]{:T(128)}, bf16[4,256,1024]{2,1,0:T(8,128)(2,1)}, s32[8,3]{1,0:T(8,128)S(1)}, bf16[8,4,32,128]{3,2,1,0:T(8,128)(2,1)}, s32[]{:T(128)}) %tuple.83), condition=%wide.while_cond, body=%wide.while_body.sunk | while | flops 2 | bytes 66677 | solution.py:147
  117.4 2.8 bitcast_dynamic-update-slice_fusion.2
  120.8 2.8 bitcast_dynamic-update-slice_fusion.2
  124.3 2.8 bitcast_dynamic-update-slice_fusion.2
  127.7 2.8 bitcast_dynamic-update-slice_fusion.2
  131.1 2.8 bitcast_dynamic-update-slice_fusion.2
  134.6 2.8 bitcast_dynamic-update-slice_fusion.2
  138.0 2.8 bitcast_dynamic-update-slice_fusion.2
  141.4 2.8 bitcast_dynamic-update-slice_fusion.2
  144.2 2.2 fusion.109
  146.5 1.4 fusion.49
  147.9 2.2 fusion.28
  150.1 1.3 copy.86
  152.8 1.4 fusion.30
  154.6 56.1 %all-reduce.2.cloned.1.call-done = f32[256,768]{1,0:T(8,128)} async-done(((f32[256,768]{1,0:T(8,128)}), f32[256,768]{1,0:T(8,128)}) %all-reduce.2.cloned.1.call-update) | async-done | bytes 786448 | tf_op jit(solution)/shard_map/psum | solution.py:203
  210.7 1.5 convert_reduce_fusion.2
  214.0 1.2 slice.185
  216.7 1.4 bitcast_convert_fusion
  218.1 1.9 copy.89
  220.7 2.7 fusion.22
  223.4 1.2 copy-done.18
  225.6 18.5 %all-gather.8.cloned.1.call-done = bf16[1024,768]{1,0:T(8,128)(2,1)} async-done(((bf16[256,768]{1,0:T(8,128)(2,1)}), bf16[1024,768]{1,0:T(8,128)(2,1)}) %all-gather.8.cloned.1.call-update) | async-done | bytes 1572880 | tf_op jit(solution)/shard_map/all_gather | solution.py:209
  244.2 2.3 convolution_convert_fusion.1
  247.4 2.5 fusion.112
  249.9 1.4 fusion.34
  251.3 2.3 copy.92
  253.7 14.3 %all-gather = f32[128,256]{1,0:T(8,128)S(1)} all-gather(f32[16,256]{1,0:T(8,128)S(1)} %get-tuple-element.197), channel_id=2, replica_groups=mesh['row'=4,'col'=8] {'col'}, dimensions={0}, use_global_device_ids=true | all-gather | bytes 147456 | tf_op jit(solution)/shard_map/all_gather | solution.py:41
  268.3 14.8 %all-gather.1 = f32[128,256]{1,0:T(8,128)S(1)} all-gather(f32[16,256]{1,0:T(8,128)S(1)} %fusion.25), channel_id=3, replica_groups=mesh['row'=4,'col'=8] {'col'}, dimensions={0}, use_global_device_ids=true | all-gather | bytes 147456 | tf_op jit(solution)/shard_map/all_gather | solution.py:41
  284.3 35.4 %all-gather.10.cloned.1.call-done = f32[8,256,768]{2,1,0:T(8,128)} async-done(((f32[1,256,768]{2,1,0:T(8,128)}), f32[8,256,768]{2,1,0:T(8,128)}) %all-gather.10.cloned.1.call-update) | async-done | bytes 6291472 | tf_op jit(solution)/shard_map/all_gather | solution.py:41
  319.7 1.2 slice_bitcast_fusion
  321.2 5.6 %slice.192 = f32[7,256,768]{2,1,0:T(8,128)} slice(f32[8,256,768]{2,1,0:T(8,128)} %all-gather.10.cloned.1.call-done), slice={[1:8], [0:256], [0:768]} | slice | bytes 11010048 | tf_op jit(solution)/shard_map/slice | solution.py:43
  326.8 32.3 %while.26 = (s32[]{:T(128)}, f32[16,256]{1,0:T(8,128)S(1)}, f32[16,256]{1,0:T(8,128)}, f32[256,768]{0,1:T(8,128)S(1)}, f32[7,16,256]{2,1,0:T(8,128)S(1)}, /*inde...) while((s32[]{:T(128)}, f32[16,256]{1,0:T(8,128)S(1)}, f32[16,256]{1,0:T(8,128)}, ...), condition=%wide.region_17.18_spmd, body=%wide.region_16.17_spmd.sunk | while | flops 618498 | bytes 6668449 | solution.py:44
  327.4 1.4 fusion.151
  328.8 1.2 constant_dynamic-slice_fusion.7
  332.0 1.4 fusion.151
  333.4 1.2 constant_dynamic-slice_fusion.7
  336.7 1.4 fusion.151
  338.0 1.2 constant_dynamic-slice_fusion.7
  341.3 1.4 fusion.151
  342.6 1.2 constant_dynamic-slice_fusion.7
  345.9 1.4 fusion.151
  347.3 1.2 constant_dynamic-slice_fusion.7
  350.5 1.4 fusion.151
  351.9 1.2 constant_dynamic-slice_fusion.7
  355.1 1.4 fusion.151
  356.5 1.2 constant_dynamic-slice_fusion.7
  359.9 1.1 copy.96
  361.4 2.1 fusion.27
  (462 shorter events, 94.9 us)
Async XLA Ops:
  7.2 354.2 %copy-start = (bf16[768,768]{1,0:T(8,128)(2,1)S(1)}, bf16[768,768]{1,0:T(8,128)(2,1)}, u32[]{:S(2)}) copy-start(bf16[768,768]{1,0:T(8,128)(2,1)} %param.35) | copy-start | bytes 3538948
  7.2 109.6 %all-gather.6.cloned.1.call-start = ((), (), s32[]{:S(2)}) async-start(), calls=%async_computation | async-start | bytes 2359296 | tf_op jit(solution)/shard_map/all_gather | solution.py:118
  7.2 1.7 copy-start.4
  11.7 1.6 copy-start.4
  16.0 1.6 copy-start.4
  20.4 1.6 copy-start.4
  22.8 1.0 copy-start.16
  24.7 1.6 copy-start.4
  27.2 1.0 copy-start.16
  29.1 1.6 copy-start.4
  31.5 1.0 copy-start.16
  33.4 1.6 copy-start.4
  37.7 1.6 copy-start.4
  42.1 1.6 copy-start.4
  44.5 1.0 copy-start.16
  46.4 1.6 copy-start.4
  50.8 1.6 copy-start.4
  55.1 1.6 copy-start.4
  59.4 1.6 copy-start.4
  61.9 1.0 copy-start.16
  63.8 1.6 copy-start.4
  68.1 1.6 copy-start.4
  70.6 1.0 copy-start.16
  72.5 1.6 copy-start.4
  75.0 1.0 copy-start.16
  80.3 2.5 copy-start.9
  80.3 2.8 copy-start.17
  80.3 2.9 copy-start.22
  80.3 8.3 %copy-start.1 = (s32[8192]{0:T(1024)S(1)}, s32[8192]{0:T(1024)}, u32[]{:S(2)}) copy-start(s32[8192]{0:T(1024)} %param.24) | copy-start | bytes 98308
  82.8 127.9 %all-reduce.2.cloned.1.call-start = ((), (), s32[]{:S(2)}) async-start(), calls=%async_computation.1 | async-start | bytes 1572864 | tf_op jit(solution)/shard_map/psum | solution.py:203
  84.3 11.5 %collective-permute-start.1 = (bf16[48,256]{1,0:T(8,128)(2,1)S(1)}, bf16[48,256]{1,0:T(8,128)(2,1)S(1)}, u32[]{:S(2)}, u32[]{:S(2)}) collective-permute-start(bf16[48,256]{1,0:T(8,128)(2,1)S(1)} %get-tuple-element.187), channel_id=1, source_target_pairs={{1,0},{2,1},{3,2},{4,3},{5,4},{6,5},{7,6},{8,7},{9,8},{10,9},{11,1... | collective-permute-start | bytes 73736 | tf_op jit(solution)/shard_map/ppermute | solution.py:33
  85.6 10.1 %collective-permute-start = (bf16[48,256]{1,0:T(8,128)(2,1)S(1)}, bf16[48,256]{1,0:T(8,128)(2,1)S(1)}, u32[]{:S(2)}, u32[]{:S(2)}) collective-permute-start(bf16[48,256]{1,0:T(8,128)(2,1)S(1)} %get-tuple-element.188), channel_id=1, source_target_pairs={{0,1},{1,2},{2,3},{3,4},{4,5},{5,6},{6,7},{7,8},{8,9},{9,10},{10,1... | collective-permute-start | bytes 73736 | tf_op jit(solution)/shard_map/ppermute | solution.py:31
  88.7 64.1 %copy-start.19 = (s32[256]{0:T(256)}, s32[256]{0:T(256)S(1)}, u32[]{:S(2)}) copy-start(s32[256]{0:T(256)S(1)} %get-tuple-element.175) | copy-start | bytes 3076
  98.8 49.1 %copy-start.11 = (bf16[8,128,128]{1,2,0:T(8,128)(2,1)S(1)}, bf16[8,128,128]{1,2,0:T(8,128)(2,1)}, u32[]{:S(2)}) copy-start(bf16[8,128,128]{1,2,0:T(8,128)(2,1)} %copy.80) | copy-start | bytes 786436
  147.9 3.8 %copy-start.25 = (bf16[128,128]{1,0:T(8,128)(2,1)S(1)}, bf16[128,128]{1,0:T(8,128)(2,1)}, u32[]{:S(2)}) copy-start(bf16[128,128]{1,0:T(8,128)(2,1)} %param.31) | copy-start | bytes 98308
  150.1 2.7 copy-start.14
  152.8 61.2 %copy-start.12 = (bf16[256,128]{1,0:T(8,128)(2,1)}, bf16[256,128]{1,0:T(8,128)(2,1)S(1)}, u32[]{:S(2)}) copy-start(bf16[256,128]{1,0:T(8,128)(2,1)S(1)} %fusion.32) | copy-start | bytes 196612
  152.8 60.2 %copy-start.21 = (f32[768]{0:T(1024)S(1)}, f32[768]{0:T(1024)}, u32[]{:S(2)}) copy-start(f32[768]{0:T(1024)} %param.33) | copy-start | bytes 9220
  154.2 89.9 %all-gather.8.cloned.1.call-start = ((), (), s32[]{:S(2)}) async-start(), calls=%async_computation.2 | async-start | bytes 1966080 | tf_op jit(solution)/shard_map/all_gather | solution.py:209
  214.0 105.7 %all-gather.10.cloned.1.call-start = ((), (), s32[]{:S(2)}) async-start(), calls=%async_computation.3 | async-start | bytes 7077888 | tf_op jit(solution)/shard_map/all_gather | solution.py:41
  223.4 1.2 copy-start.18
  225.6 21.8 %copy-start.23 = (f32[16]{0:T(128)S(1)}, f32[16]{0:T(128)}, u32[]{:S(2)}) copy-start(f32[16]{0:T(128)} %param.36) | copy-start | bytes 196
  247.4 2.5 copy-start.5
  268.0 52.9 %copy-start.6 = (f32[128,256]{1,0:T(8,128)}, f32[128,256]{1,0:T(8,128)S(1)}, u32[]{:S(2)}) copy-start(f32[128,256]{1,0:T(8,128)S(1)} %all-gather) | copy-start | bytes 393220
  321.2 5.6 %slice-start = ((f32[128,256]{1,0:T(8,128)}), f32[112,256]{1,0:T(8,128)S(1)}, s32[]{:S(2)}) async-start(f32[128,256]{1,0:T(8,128)} %copy-done.6), calls=%async_computation.4 | async-start | bytes 229376 | tf_op jit(solution)/shard_map/slice | solution.py:43
  326.8 2.0 copy-start.7
  330.3 1.1 copy-start.8
  331.4 2.0 copy-start.7
  334.9 1.1 copy-start.8
  336.0 2.0 copy-start.7
  339.5 1.1 copy-start.8
  340.6 2.0 copy-start.7
  344.1 1.1 copy-start.8
  345.2 2.0 copy-start.7
  348.7 1.1 copy-start.8
  349.8 2.0 copy-start.7
  353.3 1.1 copy-start.8
  354.5 2.0 copy-start.7
  357.9 1.1 copy-start.8
  359.1 2.3 copy-start.3
  361.3 2.1 copy-start.13
  361.4 2.1 copy-start.15
  361.4 2.1 copy-start.20
  363.5 1.1 copy-start.10
  (26 other events, 23.3 us)
Sparse Core Ops, SparseCore 0:
  82.9 33.7 all-gather.5
  154.4 56.3 all-reduce.1
  214.1 30.0 all-gather.7
  253.8 65.8 all-gather.9
where the time goes:
time: 374 us; the launch traced here: 371 us
  waiting for transfers between devices  128 us (34%)
  local copies, waits for them, and re-layouts  97.5 us (26%)
  matrix products  60 us (16%)
  other arithmetic  35.9 us (10%)
  blocking collectives  29.1 us (8%)
  between operations  14.4 us (4%)
  starting transfers between devices  4.47 us (1%)
    psum x1, waiting for transfers between devices, local(): summed = lax.psum(partial_value, 'col')  56.1 us
    all_gather x1, waiting for transfers between devices, joined(): pieces = jax.tree.map(lambda part: lax.all_gather(part, axis), value)  35.4 us
    all_gather x2, blocking collectives, joined(): pieces = jax.tree.map(lambda part: lax.all_gather(part, axis), value)  29.1 us
    gather x24, local copies, waits for them, and re-layouts  27.4 us
    dynamic_slice x32, local copies, waits for them, and re-layouts, local(): biases = lax.map(pair_step, pair_blocks).reshape(16, HB, rows_per, tok_cols)  21.3 us
    all_gather x1, waiting for transfers between devices, local(): every_token = lax.all_gather(token_normed, 'row', axis=0, tiled=True)  18.5 us
    all_gather x1, waiting for transfers between devices, local(): band_bias = lax.all_gather(atom_bias, 'col', axis=2, tiled=True)  17.9 us
    transpose x14, other arithmetic, merge_parts(): merged_out = out_early * jnp.repeat(scale_early.T, head_width, axis=1) +...  14.1 us
  transfers between devices with their start and end apart: 6, of which 4 were waited for; matrix products, arithmetic and copies ran while one was open for 6% of the time, Pallas kernels for 0%

commit v1 on v0

v1 whole, which is shorter than its diff:
```python
import functools

import jax
import jax.numpy as jnp
from jax import lax
from jax.experimental import pallas as pl
from jax.experimental.pallas import tpu as pltpu
from jax.sharding import PartitionSpec as P

CZ = 128
CS = 768
CA = 128
HT = 16
HA = 4
PH = 256
QB = 32
KW = 128
EDGE = 48
HDA = 32
HDT = 48
HB = 20

EPS = 1e-05
F32 = jnp.float32
BF16 = jnp.bfloat16


def standardize(features):
    features = features.astype(F32)
    center = features - jnp.mean(features, axis=-1, keepdims=True)
    spread = jnp.mean(center * center, axis=-1, keepdims=True)
    return center * lax.rsqrt(spread + EPS)


def dot(a, b):
    return jnp.dot(a, b, preferred_element_type=F32)


def dot_nt(a, b):
    return lax.dot_general(a, b, (((1,), (1,)), ((), ())), preferred_element_type=F32)


def pair_rows(x, up, down, heads):
    normed = standardize(x).astype(BF16)
    mixed = dot(normed, up)
    half = mixed[:, :PH]
    hidden = ((half + half * jnp.tanh(half)) * mixed[:, PH:]).astype(BF16)
    updated = x.astype(F32) + dot(hidden, down)
    return dot_nt(heads, standardize(updated).astype(BF16))


def pair_kernel(sub, x_ref, up_ref, down_ref, heads_ref, atom_ref, token_ref, stage):
    rows, cols, _ = x_ref.shape
    for at in range(0, rows, sub):
        x = x_ref[at : at + sub].reshape(sub * cols, CZ)
        found = pair_rows(x, up_ref[...], down_ref[...], heads_ref[...])
        for i in range(sub):
            stage[:, at + i, :] = found[:, i * cols : (i + 1) * cols]
    token_ref[...] = stage[:HT].astype(BF16)
    atom_ref[...] = stage[HT : HT + HA].astype(BF16)


def pair_bias(pair_tensor, pair_up, pair_down, bias_heads):
    tok_rows, tok_cols, _ = pair_tensor.shape
    tile = 16
    up = jnp.concatenate([pair_up[:, :PH] * 0.5, pair_up[:, PH:]], axis=1).astype(BF16)
    heads = jnp.zeros((32, CZ), BF16)
    heads = heads.at[:HT].set(bias_heads[:, HA:].T).at[HT : HT + HA].set(bias_heads[:, :HA].T)
    pairs = tok_rows * tok_cols
    return pl.pallas_call(
        functools.partial(pair_kernel, 4),
        grid=(tok_rows // tile,),
        in_specs=[
            pl.BlockSpec((tile, tok_cols, CZ), lambda i: (i, 0, 0)),
            pl.BlockSpec((CZ, 2 * PH), lambda i: (0, 0)),
            pl.BlockSpec((PH, CZ), lambda i: (0, 0)),
            pl.BlockSpec((32, CZ), lambda i: (0, 0)),
        ],
        out_specs=[
            pl.BlockSpec((HA, tile, tok_cols), lambda i: (0, i, 0)),
            pl.BlockSpec((HT, tile, tok_cols), lambda i: (0, i, 0)),
        ],
        out_shape=[
            jax.ShapeDtypeStruct((HA, tok_rows, tok_cols), BF16),
            jax.ShapeDtypeStruct((HT, tok_rows, tok_cols), BF16),
        ],
        scratch_shapes=[pltpu.VMEM((32, tile, tok_cols), F32)],
        compiler_params=pltpu.CompilerParams(vmem_limit_bytes=32 * 1024 * 1024),
        cost_estimate=pl.CostEstimate(
            flops=2 * pairs * (2 * CZ * PH + PH * CZ + CZ * HB),
            bytes_accessed=2 * pairs * (CZ + HB),
            transcendentals=pairs * PH,
        ),
    )(pair_tensor, up, pair_down, heads)


def with_halo(cells, axes, width):
    count = lax.axis_size(axes)
    ends = count - 1
    head, tail = cells[:width], cells[-width:]
    return jnp.concatenate(
        [
            lax.ppermute(tail, axes, [(i, i + 1) for i in range(ends)]),
            cells,
            lax.ppermute(head, axes, [(i + 1, i) for i in range(ends)]),
        ],
        axis=0,
    )


def local(
    pair_tensor,
    token_single,
    atom_single,
    atom_token,
    chain_index,
    pair_up,
    pair_down,
    bias_heads,
    atom_gain,
    atom_proj,
    atom_exit,
    atom_pool,
    token_gain,
    token_proj,
    token_exit,
    chain_bias,
    token_back,
):
    tok_rows = token_single.shape[0]
    tok_cols = pair_tensor.shape[1]
    tokens = chain_index.shape[0]
    atom_rows = atom_single.shape[0]
    atoms = atom_token.shape[0]
    col_count = lax.axis_size("col")
    row_index = lax.axis_index("row")
    col_index = lax.axis_index("col")
    row_start = row_index * tok_rows
    own = tok_rows // col_count
    own_start = row_start + col_index * own
    atom_base = (row_index * col_count + col_index) * atom_rows

    atom_normed = (standardize(atom_single) * atom_gain).astype(BF16)
    projected = dot(atom_normed, atom_proj)
    queries = projected[:, :CA].astype(BF16)
    keyvals = projected[:, CA : 3 * CA].astype(BF16)
    atom_gate = projected[:, 3 * CA :]
    extended = with_halo(keyvals, ("row", "col"), EDGE)

    atom_bias, token_bias = pair_bias(pair_tensor, pair_up, pair_down, bias_heads)
    own_bias = lax.all_to_all(token_bias, "col", split_axis=1, concat_axis=2, tiled=True)
    band = lax.all_gather(atom_bias, "col", axis=2, tiled=True)

    wide = tok_rows + 2 * tok_cols
    first_key = jnp.clip(row_start - tok_cols, 0, tokens - wide)
    band = lax.dynamic_slice_in_dim(band, first_key, wide, axis=2)
    reach = atom_rows + 2 * EDGE
    key_pos = jnp.arange(reach, dtype=jnp.int32) - EDGE
    key_tok = lax.dynamic_slice_in_dim(jnp.pad(atom_token, EDGE, mode="edge"), atom_base, reach)
    query_tok = lax.dynamic_slice_in_dim(atom_token, atom_base, atom_rows)
    block = QB * (jnp.arange(atom_rows, dtype=jnp.int32) // QB)
    valid = (
        (key_pos[None, :] >= block[:, None] - EDGE)
        & (key_pos[None, :] < block[:, None] - EDGE + KW)
        & (key_pos[None, :] + atom_base >= 0)
        & (key_pos[None, :] + atom_base < atoms)
    )
    q_hot = (query_tok[:, None] - row_start == jnp.arange(tok_rows)[None, :]).astype(BF16)
    k_hot = (key_tok[None, :] - first_key == jnp.arange(wide)[:, None]).astype(BF16)
    outs = []
    for h in range(HA):
        at = slice(h * HDA, (h + 1) * HDA)
        tile = dot(dot(q_hot, band[h]).astype(BF16), k_hot)
        scores = dot_nt(queries[:, at], extended[:, :CA][:, at]) * HDA ** (-0.5) + tile
        scores = jnp.where(valid, scores, -1e30)
        weights = jnp.exp(scores - jnp.max(scores, axis=-1, keepdims=True))
        total = jnp.sum(weights, axis=-1, keepdims=True)
        outs.append(dot(weights.astype(BF16), extended[:, CA:][:, at]) / total)
    attended = jnp.concatenate(outs, axis=1)
    atom_gated = (attended * jax.nn.sigmoid(atom_gate)).astype(BF16)
    atom_mid = (atom_single.astype(F32) + dot(atom_gated, atom_exit)).astype(BF16)

    row_mid = lax.all_gather(atom_mid, "col", axis=0, tiled=True)
    row_pooled = jax.nn.relu(dot(row_mid, atom_pool)).astype(BF16)
    row_tok = lax.dynamic_slice_in_dim(atom_token, row_index * atom_rows * col_count, atom_rows * col_count)
    pool_hot = row_tok[None, :] - own_start == jnp.arange(own)[:, None]
    counts = jnp.sum(pool_hot.astype(F32), axis=1, keepdims=True)
    pooled = dot(pool_hot.astype(BF16), row_pooled) / counts
    single = lax.dynamic_slice_in_dim(token_single, col_index * own, own)
    token_mid = (single.astype(F32) + pooled).astype(BF16)
    token_normed = (standardize(token_mid) * token_gain).astype(BF16)
    every = lax.all_gather(token_normed, ("row", "col"), axis=0, tiled=True)

    own_proj = dot(token_normed, token_proj[:, : 2 * CS])
    query = own_proj[:, :CS].astype(BF16)
    token_gate = own_proj[:, CS:]
    keyval = dot(every, token_proj[:, 2 * CS :]).astype(BF16)
    of_head = jnp.arange(CS)[None, :] // HDT == jnp.arange(HT)[:, None]
    spread = jnp.where(of_head[:, None, :], query[None], jnp.zeros((), BF16)).reshape(HT * own, CS)
    own_chain = lax.dynamic_slice_in_dim(chain_index, own_start, own)
    same = (own_chain[:, None] == chain_index[None, :]).astype(F32)
    scores = (
        (dot_nt(spread, keyval[:, :CS]) * HDT ** (-0.5)).reshape(HT, own, tokens)
        + own_bias.astype(F32)
        + chain_bias[:, None, None] * same[None]
    )
    weights = jnp.exp(scores - jnp.max(scores, axis=-1, keepdims=True))
    total = jnp.sum(weights, axis=-1, keepdims=True)
    mixed = dot(weights.astype(BF16).reshape(HT * own, tokens), keyval[:, CS:]).reshape(HT, own, CS)
    token_attended = jnp.sum(jnp.where(of_head[:, None, :], mixed / total, 0.0), axis=0)
    token_gated = (token_attended * jax.nn.sigmoid(token_gate)).astype(BF16)
    own_update = (token_mid.astype(F32) + dot(token_gated, token_exit)).astype(BF16)

    token_update = lax.all_gather(own_update, "col", axis=0, tiled=True)
    token_sent = dot(token_update, token_back).astype(BF16)
    atom_update = (atom_mid.astype(F32) + dot(q_hot, token_sent)).astype(BF16)
    return (token_update, atom_update)


def solution(mesh):
    placed = (
        P("row", "col", None),
        P("row", None),
        P(("row", "col"), None),
    ) + (P(),) * 14
    return jax.shard_map(
        local,
        mesh=mesh,
        in_specs=placed,
        out_specs=(P("row", None), P(("row", "col"), None)),
        check_vma=False,
    )
```

time: 374 us -> 224 us (0.60)
  local copies, waits for them, and re-layouts: 97.5 us -> 14.5 us
  waiting for transfers between devices: 128 us -> 67.2 us
  Pallas kernels: 0 us -> 53.1 us
  other arithmetic: 35.9 us -> 6.05 us
  matrix products: 60 us -> 30.5 us
  starting transfers between devices: 4.47 us -> 8.55 us
    psum x1 -> x0, waiting for transfers between devices: 56.1 us -> none  [local(): summed = lax.psum(partial_value, 'col')]
    pallas_call x0 -> x1, Pallas kernels: none -> 53.1 us  [pair_bias(): pl.pallas_call(functools.partial(pair_kernel, 4), grid=(tok_rows // tile,...]
    gather x25 -> x0, local copies, waits for them, and re-layouts: 33.6 us -> none
    all_gather x3 -> x2, waiting for transfers between devices: 71.9 us -> 38.6 us  [the longest x1 24.5 us: local(): band = lax.all_gather(atom_bias, 'col', axis=2, tiled=True)]
    dynamic_slice x48 -> x1, local copies, waits for them, and re-layouts: 32.9 us -> 0.07 us  [local(): own_chain = lax.dynamic_slice_in_dim(chain_index, own_start, own)]
    dot_general x60 -> x21, matrix products: 60 us -> 30.5 us  [the longest x16 23.8 us: dot(): return jnp.dot(a, b, preferred_element_type=F32)]
    all_to_all x0 -> x1, waiting for transfers between devices: none -> 27.9 us  [local(): lax.all_to_all(token_bias, 'col', split_axis=1, concat_axis=2, tiled=True)]
    transpose x14 -> x0, other arithmetic: 14.1 us -> none  [merge_parts(): merged_out = out_early * jnp.repeat(scale_early.T, head_width, axis=1) +...]
  transfers between devices with their start and end apart: 6 -> 5, of which waited for: 4 -> 4; matrix products, arithmetic and copies ran while one was open for 6% -> 6% of each run, Pallas kernels for 0% -> 0%
where the time goes in v1:
time: 224 us; the launch traced here: 223 us
  waiting for transfers between devices  67.2 us (30%)
  Pallas kernels  53.1 us (24%)
  matrix products  30.5 us (14%)
  blocking collectives  29.1 us (13%)
  local copies, waits for them, and re-layouts  14.5 us (6%)
  between operations  14.5 us (6%)
  starting transfers between devices  8.55 us (4%)
  other arithmetic  6.05 us (3%)
    pallas_call x1, Pallas kernels, pair_bias(): pl.pallas_call(functools.partial(pair_kernel, 4), grid=(tok_rows // tile,...  53.1 us
    all_to_all x1, waiting for transfers between devices, local(): lax.all_to_all(token_bias, 'col', split_axis=1, concat_axis=2, tiled=True)  27.9 us
    all_gather x1, waiting for transfers between devices, local(): band = lax.all_gather(atom_bias, 'col', axis=2, tiled=True)  24.5 us
    dot_general x16, matrix products, dot(): return jnp.dot(a, b, preferred_element_type=F32)  23.8 us
    all_gather x1, blocking collectives, local(): row_mid = lax.all_gather(atom_mid, 'col', axis=0, tiled=True)  14.7 us
    all_gather x1, blocking collectives, local(): token_update = lax.all_gather(own_update, 'col', axis=0, tiled=True)  14.4 us
    all_gather x1, waiting for transfers between devices, local(): every = lax.all_gather(token_normed, ('row', 'col'), axis=0, tiled=True)  14.1 us
    dot_general x5, matrix products, dot_nt(): lax.dot_general(a, b, (((1,), (1,)), ((), ())), preferred_element_type=F32)  6.68 us
  transfers between devices with their start and end apart: 5, of which 4 were waited for; matrix products, arithmetic and copies ran while one was open for 6% of the time, Pallas kernels for 0%

profile of v1, /device:TPU:0, one launch (start us, length us, event | category | flops | bytes accessed | tf_op | source)
XLA Modules:
  0.0 223.5 jit_solution(14842462357384916943)
XLA Ops:
  7.2 0.8 slice_bitcast_fusion.4
  8.0 0.7 constant_dynamic-update-slice_fusion.heads_ref
  8.7 0.9 slice_multiply_fusion
  9.6 3.4 %copy-done.1 = bf16[256,128,128]{2,1,0:T(8,128)(2,1)S(1)} copy-done((bf16[256,128,128]{2,1,0:T(8,128)(2,1)S(1)}, bf16[256,128,128]{2,1,0:T(8,128)(2,1)}, u32[]{:S(2)}) %copy-start.1) | copy-done | bytes 8388632
  13.0 0.8 copy-done.2
  13.8 53.1 %shard_map.176 = (bf16[4,256,128]{2,1,0:T(8,128)(2,1)}, bf16[16,256,128]{2,1,0:T(8,128)(2,1)S(1)}) custom-call(bf16[256,128,128]{2,1,0:T(8,128)(2,1)S(1)} %copy-done.1, bf16[128,512]{1,0:T(8,128)(2,1)S(1)} %pad_maximum_fusion.1.up_ref, bf16[256,128]{1,0:T(8,128)(2,1)S(1)} %copy-done.2, bf16[32,128]{1,0:T(8,128)(2,1)S(1)} %constant_dynamic-update-slice_fusion.heads_ref), custom_call_target="tpu_custom_call" | custom-call | flops 6610223104 | bytes 9699328 | tf_op jit(solution)/shard_map/pallas_call | solution.py:70
  67.0 0.1 convert_reduce_fusion.1
  67.1 0.2 fusion.50
  67.4 0.3 fusion.107
  67.6 0.6 fusion.105
  68.3 2.4 %collective-permute-start = (bf16[48,256]{1,0:T(8,128)(2,1)}, bf16[48,256]{1,0:T(8,128)(2,1)S(1)}, u32[]{:S(2)}, u32[]{:S(2)}) collective-permute-start(bf16[48,256]{1,0:T(8,128)(2,1)} %get-tuple-element.32), channel_id=1, source_target_pairs={{0,1},{1,2},{2,3},{3,4},{4,5},{5,6},{6,7},{7,8},{8,9},{9,10},{10,1... | collective-permute-start | bytes 73736 | tf_op jit(solution)/shard_map/ppermute | solution.py:103
  70.6 1.3 collective-permute-start.1
  72.0 0.6 fusion.106
  72.6 0.6 reshape.241
  73.2 0.6 reshape.240
  73.8 0.1 concatenate.19
  73.9 0.5 add_compare_fusion
  74.5 0.1 dynamic-slice_subtract_fusion.1
  74.5 0.7 convert_reduce_fusion
  75.4 0.1 copy.31
  75.5 0.6 collective-permute-done.1
  76.1 24.5 %all-gather.3.cloned.1.call-done = bf16[4,256,1024]{2,1,0:T(8,128)(2,1)} async-done(((bf16[4,256,128]{2,1,0:T(8,128)(2,1)}), bf16[4,256,1024]{2,1,0:T(8,128)(2,1)}) %all-gather.3.cloned.1.call-update) | async-done | bytes 2097168 | tf_op jit(solution)/shard_map/all_gather | solution.py:152
  100.7 2.3 %fusion.19 = f32[256,352]{0,1:T(8,128)} fusion(s32[352]{0:T(512)S(1)} %dynamic-slice_subtract_fusion.1, bf16[4,256,1024]{2,1,0:T(8,128)(2,1)} %all-gather.3.cloned.1.call-done, s32[]{:T(128)S(6)} %add.182, s32[]{:T(128)S(6)} %min.4, s32[256]{0:T(256)S(1)} %dynamic-slice_subtract_fusion.2), kind=kOutput, calls=%fused_computation.34 | convolution fusion | flops 159760384 | bytes 625032 | tf_op jit(solution)/shard_map/dot_general | solution.py:36
  102.9 1.3 fusion.109
  104.3 0.1 fusion.36
  104.3 0.3 convolution_divide_fusion.1
  104.6 2.3 %fusion.18 = f32[256,352]{0,1:T(8,128)} fusion(s32[352]{0:T(512)S(1)} %dynamic-slice_subtract_fusion.1, bf16[4,256,1024]{2,1,0:T(8,128)(2,1)} %all-gather.3.cloned.1.call-done, s32[]{:T(128)S(6)} %add.181, s32[]{:T(128)S(6)} %min.4, s32[256]{0:T(256)S(1)} %dynamic-slice_subtract_fusion.2), kind=kOutput, calls=%fused_computation.33 | convolution fusion | flops 159760384 | bytes 625032 | tf_op jit(solution)/shard_map/dot_general | solution.py:36
  106.9 1.3 fusion.110
  108.3 0.1 fusion.34
  108.4 0.3 convolution_divide_fusion.2
  108.7 2.3 %fusion.17 = f32[256,352]{0,1:T(8,128)} fusion(s32[352]{0:T(512)S(1)} %dynamic-slice_subtract_fusion.1, bf16[4,256,1024]{2,1,0:T(8,128)(2,1)} %all-gather.3.cloned.1.call-done, s32[]{:T(128)S(6)} %min.4, s32[256]{0:T(256)S(1)} %dynamic-slice_subtract_fusion.2), kind=kOutput, calls=%fused_computation.32 | convolution fusion | flops 159760384 | bytes 625028 | tf_op jit(solution)/shard_map/dot_general | solution.py:36
  111.0 1.3 fusion.111
  112.2 2.3 %fusion.20 = f32[256,352]{0,1:T(8,128)} fusion(s32[352]{0:T(512)} %copy-done.21, bf16[4,256,1024]{2,1,0:T(8,128)(2,1)} %all-gather.3.cloned.1.call-done, s32[]{:T(128)S(6)} %add.183, s32[]{:T(128)S(6)} %min.4, s32[256]{0:T(256)S(1)} %dynamic-slice_subtract_fusion.2), kind=kOutput, calls=%fused_computation.35 | convolution fusion | flops 159760384 | bytes 625672 | tf_op jit(solution)/shard_map/dot_general | solution.py:36
  114.6 1.3 fusion.108
  115.9 0.1 fusion.32
  116.0 0.2 convolution_divide_fusion.3
  116.2 0.1 fusion.38
  116.3 0.3 convolution_divide_fusion
  116.6 0.2 fusion.23
  116.8 14.7 %all_gather.13 = bf16[2048,128]{1,0:T(8,128)(2,1)S(1)} all-gather(bf16[256,128]{1,0:T(8,128)(2,1)S(1)} %fusion.23), channel_id=1, replica_groups=mesh['row'=4,'col'=8] {'col'}, dimensions={0}, use_global_device_ids=true | all-gather | bytes 589824 | tf_op jit(solution)/shard_map/all_gather | solution.py:183
  131.5 2.3 %fusion.112 = (f32[32]{0:T(128)S(1)}, f32[32,768]{1,0:T(8,128)S(1)}) fusion(f32[32]{0:T(128)S(1)} %copy-done.28, bf16[2048,128]{1,0:T(8,128)(2,1)S(1)} %all_gather.13, bf16[128,768]{1,0:T(8,128)(2,1)S(1)} %copy-done.29, s32[2048]{0:T(1024)S(1)} %dynamic-slice_subtract_fusion, bf16[256,768]{1,0:T(8,128)(2,1)} %param.22, s32[]{:T(128)S(6)} %select_n.65), kind=kOutput, calls=%fused_computation.168 | convolution fusion | flops 506675168 | bytes 876804 | tf_op jit(solution)/shard_map/dot_general | solution.py:36
  133.8 0.2 multiply_reduce_fusion
  134.0 0.7 multiply_convert_fusion
  134.8 1.7 copy.29
  136.5 4.8 %all-to-all-start = ((bf16[16,256,128]{2,0,1:T(8,128)(2,1)}), bf16[16,256,128]{2,0,1:T(8,128)(2,1)}, u32[]{:S(2)}, u32[]{:S(2)}) async-start(bf16[16,256,128]{2,0,1:T(8,128)(2,1)} %copy.29), calls=%async_computation | async-start | bytes 2097152 | tf_op jit(solution)/shard_map/all_to_all | solution.py:151
  141.4 0.7 mul.144
  142.1 0.6 iota_compare_fusion.17
  142.7 0.1 compare_convert_fusion
  142.8 27.9 %all-to-all-done = bf16[16,256,128]{2,0,1:T(8,128)(2,1)} async-done(((bf16[16,256,128]{2,0,1:T(8,128)(2,1)}), bf16[16,256,128]{2,0,1:T(8,128)(2,1)}, u32[]{:S(2)}, u32[]{:S(2)}) %all-to-all-start) | async-done | bytes 1048608 | tf_op jit(solution)/shard_map/all_to_all | solution.py:151
  170.8 1.8 copy.30
  172.6 2.2 fusion.1
  174.8 0.7 copy-done.5
  175.5 1.0 broadcast_select_fusion
  176.5 14.1 %all-gather.5.cloned.1.call-done = bf16[1024,768]{1,0:T(8,128)(2,1)} async-done(((bf16[32,768]{1,0:T(8,128)(2,1)}), bf16[1024,768]{1,0:T(8,128)(2,1)}) %all-gather.5.cloned.1.call-update) | async-done | bytes 1572880 | tf_op jit(solution)/shard_map/all_gather | solution.py:192
  190.6 4.8 %convolution_convert_fusion = bf16[1024,1536]{1,0:T(8,128)(2,1)S(1)} fusion(bf16[1024,768]{1,0:T(8,128)(2,1)} %all-gather.5.cloned.1.call-done, bf16[768,3072]{1,0:T(8,128)(2,1)} %param.34), kind=kOutput, calls=%fused_computation.1 | convolution fusion | flops 2417491968 | bytes 7077888 | tf_op jit(solution)/shard_map/dot_general | solution.py:36
  195.4 1.5 fusion.113
  196.9 0.5 fusion.5
  197.4 0.1 div.107
  197.5 0.1 copy-done.15
  197.6 2.5 %select_reduce_fusion = f32[32,768]{1,0:T(8,128)S(1)} fusion(bf16[16,32,1024]{2,1,0:T(8,128)(2,1)S(1)} %bitcast.55, bf16[1024,1536]{1,0:T(8,128)(2,1)} %copy-done.4, f32[16,32]{1,0:T(8,128)S(1)} %div.107, pred[16,768]{1,0:T(8,128)(4,1)S(1)} %copy-done.15), kind=kOutput, calls=%fused_computation.15 | convolution fusion | flops 806461440 | bytes 2734080 | tf_op jit(solution)/shard_map/dot_general | solution.py:36
  200.1 0.3 fusion.25
  200.4 14.4 %all_gather.15 = bf16[256,768]{1,0:T(8,128)(2,1)S(1)} all-gather(bf16[32,768]{1,0:T(8,128)(2,1)S(1)} %fusion.25), channel_id=1, replica_groups=mesh['row'=4,'col'=8] {'col'}, dimensions={0}, use_global_device_ids=true | all-gather | bytes 442368 | tf_op jit(solution)/shard_map/all_gather | solution.py:214
  214.8 1.1 fusion.24
  215.9 0.7 copy.36
  (88 shorter events, 0.6 us)
Async XLA Ops:
  7.2 192.9 %copy-start = (bf16[768,768]{1,0:T(8,128)(2,1)S(1)}, bf16[768,768]{1,0:T(8,128)(2,1)}, u32[]{:S(2)}) copy-start(bf16[768,768]{1,0:T(8,128)(2,1)} %param.35) | copy-start | bytes 3538948
  7.2 93.5 %all-gather.3.cloned.1.call-start = ((), (), s32[]{:S(2)}) async-start(), calls=%async_computation.1 | async-start | bytes 2359296 | tf_op jit(solution)/shard_map/all_gather | solution.py:152
  9.6 3.4 %copy-start.1 = (bf16[256,128,128]{2,1,0:T(8,128)(2,1)S(1)}, bf16[256,128,128]{2,1,0:T(8,128)(2,1)}, u32[]{:S(2)}) copy-start(bf16[256,128,128]{2,1,0:T(8,128)(2,1)} %x_ref.1) | copy-start | bytes 25165828
  13.0 0.8 copy-start.2
  13.8 53.2 %copy-start.7 = (bf16[256,128]{1,0:T(8,128)(2,1)S(1)}, bf16[256,128]{1,0:T(8,128)(2,1)}, u32[]{:S(2)}) copy-start(bf16[256,128]{1,0:T(8,128)(2,1)} %param.23) | copy-start | bytes 196612
  13.8 53.5 %copy-start.12 = (bf16[128,512]{1,0:T(8,128)(2,1)S(1)}, bf16[128,512]{1,0:T(8,128)(2,1)}, u32[]{:S(2)}) copy-start(bf16[128,512]{1,0:T(8,128)(2,1)} %param.30) | copy-start | bytes 393220
  13.8 53.5 %copy-start.26 = (f32[128]{0:T(128)S(1)}, f32[128]{0:T(128)}, u32[]{:S(2)}) copy-start(f32[128]{0:T(128)} %param.29) | copy-start | bytes 1540
  13.8 58.1 %copy-start.13 = (s32[8192]{0:T(1024)S(1)}, s32[8192]{0:T(1024)}, u32[]{:S(2)}) copy-start(s32[8192]{0:T(1024)} %param.24) | copy-start | bytes 98308
  67.0 123.6 %all-gather.5.cloned.1.call-start = ((), (), s32[]{:S(2)}) async-start(), calls=%async_computation.2 | async-start | bytes 1622016 | tf_op jit(solution)/shard_map/all_gather | solution.py:192
  68.3 7.2 %collective-permute-start = (bf16[48,256]{1,0:T(8,128)(2,1)}, bf16[48,256]{1,0:T(8,128)(2,1)S(1)}, u32[]{:S(2)}, u32[]{:S(2)}) collective-permute-start(bf16[48,256]{1,0:T(8,128)(2,1)} %get-tuple-element.32), channel_id=1, source_target_pairs={{0,1},{1,2},{2,3},{3,4},{4,5},{5,6},{6,7},{7,8},{8,9},{9,10},{10,1... | collective-permute-start | bytes 73736 | tf_op jit(solution)/shard_map/ppermute | solution.py:103
  70.6 5.5 %collective-permute-start.1 = (bf16[48,256]{1,0:T(8,128)(2,1)}, bf16[48,256]{1,0:T(8,128)(2,1)S(1)}, u32[]{:S(2)}, u32[]{:S(2)}) collective-permute-start(bf16[48,256]{1,0:T(8,128)(2,1)} %get-tuple-element.33), channel_id=1, source_target_pairs={{1,0},{2,1},{3,2},{4,3},{5,4},{6,5},{7,6},{8,7},{9,8},{10,9},{11,1... | collective-permute-start | bytes 73736 | tf_op jit(solution)/shard_map/ppermute | solution.py:105
  74.4 32.5 %copy-start.31 = (pred[352]{0:T(512)(128)(4,1)}, pred[352]{0:T(512)(128)(4,1)S(1)}, u32[]{:S(2)}) copy-start(pred[352]{0:T(512)(128)(4,1)S(1)} %get-tuple-element.54) | copy-start | bytes 1060
  74.4 32.5 %copy-start.22 = (s32[256]{0:T(256)}, s32[256]{0:T(256)S(1)}, u32[]{:S(2)}) copy-start(s32[256]{0:T(256)S(1)} %get-tuple-element.52) | copy-start | bytes 3076
  74.4 32.5 %copy-start.24 = (s32[256]{0:T(256)}, s32[256]{0:T(256)S(1)}, u32[]{:S(2)}) copy-start(s32[256]{0:T(256)S(1)} %get-tuple-element.53) | copy-start | bytes 3076
  74.5 34.1 %copy-start.21 = (s32[352]{0:T(512)}, s32[352]{0:T(512)S(1)}, u32[]{:S(2)}) copy-start(s32[352]{0:T(512)S(1)} %dynamic-slice_subtract_fusion.1) | copy-start | bytes 4228
  75.3 36.9 %copy-start.17 = (s32[256]{0:T(256)}, s32[256]{0:T(256)S(1)}, u32[]{:S(2)}) copy-start(s32[256]{0:T(256)S(1)} %dynamic-slice_subtract_fusion.2) | copy-start | bytes 3076
  75.4 31.5 %copy-start.33 = (pred[352]{0:T(512)(128)(4,1)S(1)}, pred[352]{0:T(512)(128)(4,1)}, u32[]{:S(2)}) copy-start(pred[352]{0:T(512)(128)(4,1)} %get-tuple-element.55) | copy-start | bytes 1060
  104.2 6.7 %copy-start.34 = (pred[352]{0:T(512)(128)(4,1)S(1)}, pred[352]{0:T(512)(128)(4,1)}, u32[]{:S(2)}) copy-start(pred[352]{0:T(512)(128)(4,1)} %get-tuple-element.55) | copy-start | bytes 1060
  108.2 6.3 %copy-start.23 = (s32[256]{0:T(256)S(1)}, s32[256]{0:T(256)}, u32[]{:S(2)}) copy-start(s32[256]{0:T(256)} %copy-done.22) | copy-start | bytes 3076
  108.3 6.3 %copy-start.25 = (s32[256]{0:T(256)S(1)}, s32[256]{0:T(256)}, u32[]{:S(2)}) copy-start(s32[256]{0:T(256)} %copy-done.24) | copy-start | bytes 3076
  108.3 6.3 %copy-start.32 = (pred[352]{0:T(512)(128)(4,1)S(1)}, pred[352]{0:T(512)(128)(4,1)}, u32[]{:S(2)}) copy-start(pred[352]{0:T(512)(128)(4,1)} %copy-done.31) | copy-start | bytes 1060
  110.9 5.6 %copy-start.30 = (bf16[128,128]{1,0:T(8,128)(2,1)S(1)}, bf16[128,128]{1,0:T(8,128)(2,1)}, u32[]{:S(2)}) copy-start(bf16[128,128]{1,0:T(8,128)(2,1)} %param.31) | copy-start | bytes 98308
  114.6 17.0 %copy-start.28 = (f32[32]{0:T(128)S(1)}, f32[32]{0:T(128)}, u32[]{:S(2)}) copy-start(f32[32]{0:T(128)} %convert_reduce_fusion) | copy-start | bytes 388
  115.9 15.6 %copy-start.29 = (bf16[128,768]{1,0:T(8,128)(2,1)S(1)}, bf16[128,768]{1,0:T(8,128)(2,1)}, u32[]{:S(2)}) copy-start(bf16[128,768]{1,0:T(8,128)(2,1)} %param.32) | copy-start | bytes 589828
  116.6 17.5 %copy-start.19 = (f32[768]{0:T(1024)S(1)}, f32[768]{0:T(1024)}, u32[]{:S(2)}) copy-start(f32[768]{0:T(1024)} %param.33) | copy-start | bytes 9220
  116.8 19.7 %copy-start.9 = (bf16[256,128]{1,0:T(8,128)(2,1)}, bf16[256,128]{1,0:T(8,128)(2,1)S(1)}, u32[]{:S(2)}) copy-start(bf16[256,128]{1,0:T(8,128)(2,1)S(1)} %fusion.23) | copy-start | bytes 196612
  134.8 6.5 %copy-start.27 = (f32[16]{0:T(128)S(1)}, f32[16]{0:T(128)}, u32[]{:S(2)}) copy-start(f32[16]{0:T(128)} %param.36) | copy-start | bytes 196
  134.8 7.3 %copy-start.20 = (s32[1024]{0:T(1024)S(1)}, s32[1024]{0:T(1024)}, u32[]{:S(2)}) copy-start(s32[1024]{0:T(1024)} %param.25) | copy-start | bytes 12292
  136.5 34.3 %all-to-all-start = ((bf16[16,256,128]{2,0,1:T(8,128)(2,1)}), bf16[16,256,128]{2,0,1:T(8,128)(2,1)}, u32[]{:S(2)}, u32[]{:S(2)}) async-start(bf16[16,256,128]{2,0,1:T(8,128)(2,1)} %copy.29), calls=%async_computation | async-start | bytes 2097152 | tf_op jit(solution)/shard_map/all_to_all | solution.py:151
  141.3 31.3 %copy-start.8 = (bf16[32,768]{1,0:T(8,128)(2,1)S(1)}, bf16[32,768]{1,0:T(8,128)(2,1)}, u32[]{:S(2)}) copy-start(bf16[32,768]{1,0:T(8,128)(2,1)} %multiply_convert_fusion) | copy-start | bytes 147460
  172.6 2.9 %copy-start.14 = (pred[16,768]{1,0:T(8,128)(4,1)S(1)}, pred[16,768]{1,0:T(8,128)(4,1)}, u32[]{:S(2)}) copy-start(pred[16,768]{1,0:T(8,128)(4,1)} %iota_compare_fusion.17) | copy-start | bytes 36868
  174.8 0.7 copy-start.5
  176.5 18.9 %copy-start.16 = (f32[512]{0:T(512)S(1)}, f32[512]{0:T(512)}, u32[]{:S(2)}) copy-start(f32[512]{0:T(512)} %mul.144) | copy-start | bytes 6148
  190.6 4.8 %copy-start.3 = (bf16[16,32,768]{2,1,0:T(8,128)(2,1)S(1)}, bf16[16,32,768]{2,1,0:T(8,128)(2,1)}, u32[]{:S(2)}) copy-start(bf16[16,32,768]{2,1,0:T(8,128)(2,1)} %broadcast_select_fusion) | copy-start | bytes 2359300
  195.4 2.0 copy-start.4
  196.9 0.7 copy-start.15
  197.6 2.5 %copy-start.6 = (f32[32,1536]{1,0:T(8,128)S(1)}, f32[32,1536]{1,0:T(8,128)}, u32[]{:S(2)}) copy-start(f32[32,1536]{1,0:T(8,128)} %copy-done.5) | copy-start | bytes 589828
  197.6 17.2 %copy-start.10 = (bf16[256,128]{1,0:T(8,128)(2,1)S(1)}, bf16[256,128]{1,0:T(8,128)(2,1)}, u32[]{:S(2)}) copy-start(bf16[256,128]{1,0:T(8,128)(2,1)} %copy-done.9) | copy-start | bytes 196612
  197.6 17.2 %copy-start.11 = (bf16[768,128]{1,0:T(8,128)(2,1)S(1)}, bf16[768,128]{1,0:T(8,128)(2,1)}, u32[]{:S(2)}) copy-start(bf16[768,128]{1,0:T(8,128)(2,1)} %param.37) | copy-start | bytes 589828
  197.6 17.2 %copy-start.18 = (s32[256]{0:T(256)S(1)}, s32[256]{0:T(256)}, u32[]{:S(2)}) copy-start(s32[256]{0:T(256)} %copy-done.17) | copy-start | bytes 3076
Sparse Core Ops, SparseCore 0:
  67.1 33.5 all-gather.2
  134.9 55.6 all-gather.4

commit v2 on v1

v2 whole, which is shorter than its diff:
```python
import functools

import jax
import jax.numpy as jnp
from jax import lax
from jax.experimental import pallas as pl
from jax.experimental.pallas import tpu as pltpu
from jax.sharding import PartitionSpec as P

CZ = 128
CS = 768
CA = 128
HT = 16
HA = 4
PH = 256
QB = 32
KW = 128
EDGE = 48
HDA = 32
HDT = 48
HB = 20

EPS = 1e-05
F32 = jnp.float32
BF16 = jnp.bfloat16


def standardize(features):
    features = features.astype(F32)
    center = features - jnp.mean(features, axis=-1, keepdims=True)
    spread = jnp.mean(center * center, axis=-1, keepdims=True)
    return center * lax.rsqrt(spread + EPS)


def dot(a, b):
    return jnp.dot(a, b, preferred_element_type=F32)


def dot_nt(a, b):
    return lax.dot_general(a, b, (((1,), (1,)), ((), ())), preferred_element_type=F32)


def pair_up_part(x, up):
    return dot(standardize(x).astype(BF16), up)


def pair_down_part(x, mixed, down):
    half = mixed[:, :PH]
    hidden = ((half + half * jnp.tanh(half)) * mixed[:, PH:]).astype(BF16)
    return x.astype(F32) + dot(hidden, down)


def pair_kernel(sub, x_ref, up_ref, down_ref, heads_ref, atom_ref, token_ref, stage):
    rows, cols, _ = x_ref.shape
    groups = rows // sub

    def load(g):
        return x_ref[g * sub : (g + 1) * sub].reshape(sub * cols, CZ)

    mixed, updated = {}, {}
    for step in range(groups + 2):
        if step < groups:
            mixed[step] = pair_up_part(load(step), up_ref[...])
        g = step - 1
        if 0 <= g < groups:
            updated[g] = pair_down_part(load(g), mixed.pop(g), down_ref[...])
        g = step - 2
        if 0 <= g < groups:
            found = dot_nt(heads_ref[...], standardize(updated.pop(g)).astype(BF16))
            for i in range(sub):
                stage[:, g * sub + i, :] = found[:, i * cols : (i + 1) * cols]
    token_ref[...] = stage[:HT].astype(BF16)
    atom_ref[...] = stage[HT : HT + HA].astype(BF16)


def pair_bias(pair_tensor, pair_up, pair_down, bias_heads):
    tok_rows, tok_cols, _ = pair_tensor.shape
    tile = 32
    up = jnp.concatenate([pair_up[:, :PH] * 0.5, pair_up[:, PH:]], axis=1).astype(BF16)
    heads = jnp.zeros((32, CZ), BF16)
    heads = heads.at[:HT].set(bias_heads[:, HA:].T).at[HT : HT + HA].set(bias_heads[:, :HA].T)
    pairs = tok_rows * tok_cols
    return pl.pallas_call(
        functools.partial(pair_kernel, 2),
        grid=(tok_rows // tile,),
        in_specs=[
            pl.BlockSpec((tile, tok_cols, CZ), lambda i: (i, 0, 0)),
            pl.BlockSpec((CZ, 2 * PH), lambda i: (0, 0)),
            pl.BlockSpec((PH, CZ), lambda i: (0, 0)),
            pl.BlockSpec((32, CZ), lambda i: (0, 0)),
        ],
        out_specs=[
            pl.BlockSpec((HA, tile, tok_cols), lambda i: (0, i, 0)),
            pl.BlockSpec((HT, tile, tok_cols), lambda i: (0, i, 0)),
        ],
        out_shape=[
            jax.ShapeDtypeStruct((HA, tok_rows, tok_cols), BF16),
            jax.ShapeDtypeStruct((HT, tok_rows, tok_cols), BF16),
        ],
        scratch_shapes=[pltpu.VMEM((32, tile, tok_cols), F32)],
        compiler_params=pltpu.CompilerParams(vmem_limit_bytes=32 * 1024 * 1024),
        cost_estimate=pl.CostEstimate(
            flops=2 * pairs * (2 * CZ * PH + PH * CZ + CZ * HB),
            bytes_accessed=2 * pairs * (CZ + HB),
            transcendentals=pairs * PH,
        ),
    )(pair_tensor, up, pair_down, heads)


FAR = 1 << 20
MESH = pl.DeviceIdType.MESH


def after_kernel(
    nrow,
    ncol,
    atom_bias,
    token_bias,
    proj_hbm,
    exit_hbm,
    queries,
    atom_gate,
    keys,
    vals,
    atom_single,
    query_tok,
    key_tok,
    row_tok,
    own_chain,
    all_chain,
    single,
    of_head,
    atom_exit,
    atom_pool,
    token_gain,
    chain_rows,
    token_back,
    token_out,
    atom_out,
    band,
    own_bias,
    mids,
    every,
    updates,
    proj,
    exit_w,
    local_sem,
    band_send,
    band_pass,
    band_recv,
    bias_sem,
    mid_sem,
    tok_send,
    tok_recv,
    pass_send,
    pass_recv,
    upd_sem,
):
    r, c = lax.axis_index("row"), lax.axis_index("col")
    side = lax.rem(c, 2)
    partner = c + 1 - 2 * side
    half = ncol // 2
    tok_rows, tok_cols = band.shape[2:]
    slots = band.shape[0]
    ratio = tok_rows // tok_cols
    own = single.shape[0]
    atom_rows = queries.shape[0]
    tokens = all_chain.shape[1]

    def send(src, dst, send_sem, recv_sem, row, col):
        return pltpu.make_async_remote_copy(
            src_ref=src,
            dst_ref=dst,
            send_sem=send_sem,
            recv_sem=recv_sem,
            device_id=(row, col),
            device_id_type=MESH,
        )

    barrier = pltpu.get_barrier_semaphore()
    for k in range(1, ncol):
        pl.semaphore_signal(barrier, inc=1, device_id=(r, lax.rem(c + k, ncol)), device_id_type=MESH)
    for k in range(1, nrow):
        pl.semaphore_signal(barrier, inc=1, device_id=(lax.rem(r + k, nrow), c), device_id_type=MESH)

    loads = [
        pltpu.make_async_copy(proj_hbm, proj, local_sem.at[0]),
        pltpu.make_async_copy(exit_hbm, exit_w, local_sem.at[1]),
        pltpu.make_async_copy(
            token_bias.at[:, pl.ds(pl.multiple_of(c * own, own), own), :], own_bias.at[c], local_sem.at[2]
        ),
    ]
    for load in loads:
        load.start()

    def span(s):
        at = (s - 1) * tok_cols
        reach = QB + EDGE - 1
        low = max(0, at - reach) // 16 * 16
        high = min(tok_rows, -(-(at + tok_cols + reach) // 16) * 16)
        return low, high

    def source(s):
        col = r * ratio + s - 1
        return col, (col >= 0) & (col < ncol)

    for s in range(slots):
        low, high = span(s)
        if low > 0:
            band[s, :, 0:low, :] = jnp.zeros((HA, low, tok_cols), BF16)
        if high < tok_rows:
            band[s, :, high:tok_rows, :] = jnp.zeros((HA, tok_rows - high, tok_cols), BF16)

    pl.semaphore_wait(barrier, ncol - 1 + nrow - 1)

    def block(s):
        low, high = span(s)
        return band.at[s, :, pl.ds(low, high - low), :]

    def from_source(s, k):
        low, high = span(s)
        col = partner if k == 0 else lax.rem(c + 2 * k, ncol)
        return send(
            atom_bias.at[:, pl.ds(low, high - low), :], block(s), band_send.at[k], band_recv.at[s], r, col
        )

    def passed(s):
        return send(block(s), block(s), band_pass.at[s], band_recv.at[s], r, partner)

    def kept(s):
        low, high = span(s)
        return pltpu.make_async_copy(atom_bias.at[:, pl.ds(low, high - low), :], block(s), local_sem.at[3])

    for s in range(slots):
        col, there = source(s)

        @pl.when(c == col)
        def _():
            for k in list(range(1, half)) + [0]:
                from_source(s, k).start()
            kept(s).start()

        @pl.when(jnp.logical_not(there))
        def _():
            low, high = span(s)
            band[s, :, low:high, :] = jnp.zeros((HA, high - low, tok_cols), BF16)

    for s in range(slots):
        col, there = source(s)

        @pl.when(there & (c != col) & (lax.rem(col + 2, 2) == side))
        def _():
            passed(s).wait_recv()
            passed(s).start()

    for s in range(slots):
        col, there = source(s)

        @pl.when(there & (lax.rem(col + 2, 2) != side))
        def _():
            passed(s).wait_recv()

        @pl.when(c == col)
        def _():
            kept(s).wait()

    biases = []
    for k in range(1, ncol):
        col = lax.rem(c + k, ncol)
        biases.append(
            send(
                token_bias.at[:, pl.ds(pl.multiple_of(col * own, own), own), :],
                own_bias.at[c],
                bias_sem.at[0, k],
                bias_sem.at[1, k],
                r,
                col,
            )
        )
        biases[-1].start()

    padded = keys.shape[0]
    q_iota = lax.broadcasted_iota(jnp.int32, (atom_rows, padded), 0)
    k_iota = lax.broadcasted_iota(jnp.int32, (atom_rows, padded), 1) - EDGE
    first = jnp.bitwise_and(q_iota, -QB) - EDGE
    valid = (k_iota >= first) & (k_iota < first + KW) & (key_tok[...] > -FAR // 2)
    q_hot = (query_tok[...] == lax.broadcasted_iota(jnp.int32, (atom_rows, tok_rows), 1)).astype(F32).astype(BF16)
    k_hot = (key_tok[...] == lax.broadcasted_iota(jnp.int32, (slots * tok_cols, padded), 0)).astype(F32).astype(BF16)
    lane = lax.broadcasted_iota(jnp.int32, (1, CA), 1)
    attended = jnp.zeros((atom_rows, CA), F32)
    for h in range(HA):
        mine = ((lane >= h * HDA) & (lane < (h + 1) * HDA)).astype(F32)
        wide = jnp.concatenate([band[s, h] for s in range(slots)], axis=1)
        tile = dot(dot(q_hot, wide).astype(BF16), k_hot)
        query = (queries[...].astype(F32) * mine).astype(BF16)
        scores = dot_nt(query, keys[...]) * HDA ** (-0.5) + tile
        scores = jnp.where(valid, scores, -1e30)
        weights = jnp.exp(scores - jnp.max(scores, axis=-1, keepdims=True))
        total = jnp.sum(weights, axis=-1, keepdims=True)
        attended += dot(weights.astype(BF16), vals[...]) / total * mine
    atom_gated = (attended * jax.nn.sigmoid(atom_gate[...])).astype(BF16)
    atom_mid = (atom_single[...].astype(F32) + dot(atom_gated, atom_exit[...])).astype(BF16)
    mids[c] = atom_mid

    def gather_start(buf, sems):
        out = [send(buf.at[c], buf.at[c], sems.at[0, k], sems.at[1, k], r, lax.rem(c + 2 * k, ncol)) for k in range(1, half)]
        over = [send(buf.at[c], buf.at[c], sems.at[2, 0], sems.at[3, 0], r, partner)]
        for copy in out + over:
            copy.start()
        return out, over

    def gather_end(buf, sems, out, over):
        for k in range(1, half):
            out[k - 1].wait_recv()
            col = lax.rem(c + ncol - 2 * k, ncol)
            over.append(send(buf.at[col], buf.at[col], sems.at[2, k], sems.at[3, k], r, partner))
            over[-1].start()
        for copy in over:
            copy.wait_recv()

    out, over = gather_start(mids, mid_sem)
    sent = out + over
    gather_end(mids, mid_sem, out, over)
    sent = out + over

    row_pooled = jax.nn.relu(dot(mids[...].reshape(ncol * atom_rows, CA), atom_pool[...])).astype(BF16)
    pool_hot = (row_tok[...] == lax.broadcasted_iota(jnp.int32, (own, ncol * atom_rows), 0)).astype(F32)
    counts = jnp.sum(pool_hot, axis=1, keepdims=True)
    pooled = dot(pool_hot.astype(BF16), row_pooled) / counts
    token_mid = (single[...].astype(F32) + pooled).astype(BF16)
    token_normed = (standardize(token_mid) * token_gain[...]).astype(BF16)
    every[r, c] = token_normed

    def piece(row, col):
        return every.at[row, col]

    def along(k):
        return send(piece(r, c), piece(r, c), tok_send.at[k, 0], tok_recv.at[k, 0], r, lax.rem(c + 2 * k, ncol))

    def across(k, j):
        col = lax.rem(c + ncol - 2 * k, ncol)
        return send(piece(r, col), piece(r, col), tok_send.at[k, j], tok_recv.at[k, j], lax.rem(r + j, nrow), c)

    def over_to(k, j):
        col = lax.rem(c + ncol - 2 * k, ncol)
        row = lax.rem(r + nrow - j, nrow)
        return send(piece(row, col), piece(row, col), pass_send.at[k, j], pass_recv.at[k, j], r, partner)

    for k in range(1, half):
        along(k).start()
    for k in range(half):
        if k > 0:
            along(k).wait_recv()
        for j in range(1, nrow):
            across(k, j).start()
        over_to(k, 0).start()
    loads[0].wait()
    own_proj = dot(token_normed, proj[:, : 2 * CS])
    query = own_proj[:, :CS].astype(BF16)
    token_gate = own_proj[:, CS:]
    for k in range(half):
        for j in range(1, nrow):
            across(k, j).wait_recv()
            over_to(k, j).start()
    for k in range(half):
        for j in range(nrow):
            over_to(k, j).wait_recv()

    keyval = dot(every[...].reshape(tokens, CS), proj[:, 2 * CS :]).astype(BF16)
    spread = jnp.concatenate([query] * HT, axis=0) * of_head[...]
    same = (own_chain[...] == all_chain[...]).astype(F32)
    same = jnp.concatenate([same] * HT, axis=0) * chain_rows[...]
    loads[2].wait()
    for copy in biases:
        copy.wait_recv()
    bias = jnp.concatenate([own_bias[k].reshape(HT * own, tok_cols) for k in range(ncol)], axis=1)
    scores = dot_nt(spread, keyval[:, :CS]) * HDT ** (-0.5) + bias.astype(F32) + same
    weights = jnp.exp(scores - jnp.max(scores, axis=-1, keepdims=True))
    total = jnp.sum(weights, axis=-1, keepdims=True)
    mixed = dot(weights.astype(BF16), keyval[:, CS:]) / total * of_head[...].astype(F32)
    token_attended = jnp.sum(mixed.reshape(HT, own, CS), axis=0)
    token_gated = (token_attended * jax.nn.sigmoid(token_gate)).astype(BF16)
    loads[1].wait()
    updates[c] = (token_mid.astype(F32) + dot(token_gated, exit_w[...])).astype(BF16)

    out, over = gather_start(updates, upd_sem)
    gather_end(updates, upd_sem, out, over)
    sent = sent + out + over
    token_out[...] = updates[...]
    token_sent = dot(updates[...].reshape(tok_rows, CS), token_back[...]).astype(BF16)
    atom_out[...] = (atom_mid.astype(F32) + dot(q_hot, token_sent)).astype(BF16)

    for copy in sent + biases:
        copy.wait_send()
    for k in range(half):
        if k > 0:
            along(k).wait_send()
        for j in range(1, nrow):
            across(k, j).wait_send()
        for j in range(nrow):
            over_to(k, j).wait_send()
    for s in range(slots):
        col, there = source(s)

        @pl.when(c == col)
        def _():
            for k in range(half):
                from_source(s, k).wait_send()

        @pl.when(there & (c != col) & (lax.rem(col + 2, 2) == side))
        def _():
            passed(s).wait_send()


def with_halo(cells, axes, width):
    count = lax.axis_size(axes)
    ends = count - 1
    head, tail = cells[:width], cells[-width:]
    return jnp.concatenate(
        [
            lax.ppermute(tail, axes, [(i, i + 1) for i in range(ends)]),
            cells,
            lax.ppermute(head, axes, [(i + 1, i) for i in range(ends)]),
        ],
        axis=0,
    )


def local(
    pair_tensor,
    token_single,
    atom_single,
    atom_token,
    chain_index,
    pair_up,
    pair_down,
    bias_heads,
    atom_gain,
    atom_proj,
    atom_exit,
    atom_pool,
    token_gain,
    token_proj,
    token_exit,
    chain_bias,
    token_back,
):
    tok_rows = token_single.shape[0]
    tok_cols = pair_tensor.shape[1]
    atom_rows = atom_single.shape[0]
    col_count = lax.axis_size("col")
    row_index = lax.axis_index("row")
    col_index = lax.axis_index("col")
    row_start = row_index * tok_rows
    own = tok_rows // col_count
    own_start = row_start + col_index * own
    atom_base = (row_index * col_count + col_index) * atom_rows

    atom_normed = (standardize(atom_single) * atom_gain).astype(BF16)
    projected = dot(atom_normed, atom_proj)
    queries = projected[:, :CA].astype(BF16)
    keyvals = projected[:, CA : 3 * CA].astype(BF16)
    atom_gate = projected[:, 3 * CA :]
    extended = with_halo(keyvals, ("row", "col"), EDGE)

    atom_bias, token_bias = pair_bias(pair_tensor, pair_up, pair_down, bias_heads)

    reach = atom_rows + 2 * EDGE
    padded = -(-reach // 128) * 128
    grown = jnp.pad(extended, ((0, padded - reach), (0, 0)))
    near = jnp.pad(atom_token, (EDGE, EDGE + padded - reach), constant_values=-FAR)
    key_tok = lax.dynamic_slice_in_dim(near, atom_base, padded) - (row_start - tok_cols)
    query_tok = lax.dynamic_slice_in_dim(atom_token, atom_base, atom_rows) - row_start
    row_atoms = atom_rows * col_count
    row_tok = lax.dynamic_slice_in_dim(atom_token, row_index * row_atoms, row_atoms) - own_start
    own_chain = lax.dynamic_slice_in_dim(chain_index, own_start, own)
    single = lax.dynamic_slice_in_dim(token_single, col_index * own, own)
    of_head = jnp.arange(CS)[None, :] // HDT == jnp.arange(HT * own)[:, None] // own
    row_count = lax.axis_size("row")
    slots = tok_rows // tok_cols + 2
    half = col_count // 2
    vmem = pl.BlockSpec(memory_space=pltpu.VMEM)
    anywhere = pl.BlockSpec(memory_space=pl.ANY)
    dma = pltpu.SemaphoreType.DMA
    token_update, atom_update = pl.pallas_call(
        functools.partial(after_kernel, row_count, col_count),
        in_specs=[anywhere] * 4 + [vmem] * 17,
        out_specs=[vmem, vmem],
        out_shape=[
            jax.ShapeDtypeStruct((col_count, own, CS), BF16),
            jax.ShapeDtypeStruct((atom_rows, CA), BF16),
        ],
        scratch_shapes=[
            pltpu.VMEM((slots, HA, tok_rows, tok_cols), BF16),
            pltpu.VMEM((col_count, HT, own, tok_cols), BF16),
            pltpu.VMEM((col_count, atom_rows, CA), BF16),
            pltpu.VMEM((row_count, col_count, own, CS), BF16),
            pltpu.VMEM((col_count, own, CS), BF16),
            pltpu.VMEM(token_proj.shape, BF16),
            pltpu.VMEM(token_exit.shape, BF16),
            dma((4,)),
            dma((half,)),
            dma((slots,)),
            dma((slots,)),
            dma((2, col_count)),
            dma((4, half)),
            dma((half, row_count)),
            dma((half, row_count)),
            dma((half, row_count)),
            dma((half, row_count)),
            dma((4, half)),
        ],
        compiler_params=pltpu.CompilerParams(
            collective_id=0, has_side_effects=True, vmem_limit_bytes=52 * 1024 * 1024
        ),
    )(
        atom_bias,
        token_bias,
        token_proj,
        token_exit,
        queries,
        atom_gate,
        grown[:, :CA],
        grown[:, CA:],
        atom_single,
        query_tok[:, None],
        key_tok[None, :],
        row_tok[None, :],
        own_chain[:, None],
        chain_index[None, :],
        single,
        of_head.astype(BF16),
        atom_exit,
        atom_pool,
        token_gain[None, :],
        jnp.repeat(chain_bias, own)[:, None],
        token_back,
    )
    return (token_update.reshape(tok_rows, CS), atom_update)


def solution(mesh):
    placed = (
        P("row", "col", None),
        P("row", None),
        P(("row", "col"), None),
    ) + (P(),) * 14
    return jax.shard_map(
        local,
        mesh=mesh,
        in_specs=placed,
        out_specs=(P("row", None), P(("row", "col"), None)),
        check_vma=False,
    )
```

time: 224 us -> 146 us (0.65)
  Pallas kernels: 53.1 us -> 125 us
  waiting for transfers between devices: 67.2 us -> 0.01 us
  matrix products: 30.5 us -> 1.24 us
  blocking collectives: 29.1 us -> 0 us
  between operations: 14.5 us -> 0.9 us
  local copies, waits for them, and re-layouts: 14.5 us -> 9.11 us
  starting transfers between devices: 8.55 us -> 3.65 us
    pallas_call x1 -> x2, Pallas kernels: 53.1 us -> 125 us  [the longest x1 85.4 us: local(): pl.pallas_call(functools.partial(after_kernel, row_count, col_count), in_...]
    all_gather x2 -> x0, waiting for transfers between devices: 38.6 us -> none  [the longest x1 24.5 us: local(): band = lax.all_gather(atom_bias, 'col', axis=2, tiled=True)]
    all_gather x2 -> x0, blocking collectives: 29.1 us -> none  [the longest x1 14.7 us: local(): row_mid = lax.all_gather(atom_mid, 'col', axis=0, tiled=True)]
    all_to_all x1 -> x0, waiting for transfers between devices: 27.9 us -> none  [local(): lax.all_to_all(token_bias, 'col', split_axis=1, concat_axis=2, tiled=True)]
    dot_general x16 -> x1, matrix products: 23.8 us -> 1.24 us  [dot(): return jnp.dot(a, b, preferred_element_type=F32)]
    dot_general x5 -> x0, matrix products: 6.68 us -> none  [dot_nt(): lax.dot_general(a, b, (((1,), (1,)), ((), ())), preferred_element_type=F32)]
    all_to_all x1 -> x0, starting transfers between devices: 4.81 us -> none  [local(): lax.all_to_all(token_bias, 'col', split_axis=1, concat_axis=2, tiled=True)]
    unnamed x72 -> x26, local copies, waits for them, and re-layouts: 6.01 us -> 7.01 us
  transfers between devices with their start and end apart: 5 -> 2, of which waited for: 4 -> 0; matrix products, arithmetic and copies ran while one was open for 6% -> 4% of each run, Pallas kernels for 0% -> 27%
where the time goes in v2:
time: 146 us; the launch traced here: 145 us
  Pallas kernels  125 us (86%)
  local copies, waits for them, and re-layouts  9.11 us (6%)
  other arithmetic  5.63 us (4%)
  starting transfers between devices  3.65 us (2%)
    pallas_call x1, Pallas kernels, local(): pl.pallas_call(functools.partial(after_kernel, row_count, col_count), in_...  85.4 us
    pallas_call x1, Pallas kernels, pair_bias(): pl.pallas_call(functools.partial(pair_kernel, 2), grid=(tok_rows // tile,...  39.2 us
    unnamed x26, local copies, waits for them, and re-layouts  7.01 us
  transfers between devices with their start and end apart: 2, of which 0 were waited for; matrix products, arithmetic and copies ran while one was open for 4% of the time, Pallas kernels for 27%

profile of v2, /device:TPU:0, one launch (start us, length us, event | category | flops | bytes accessed | tf_op | source)
XLA Modules:
  0.0 145.1 jit_solution(17297532896813356887)
XLA Ops:
  0.6 0.0 copy-start
  0.6 0.0 copy-start.9
  0.7 0.0 copy-start.8
  0.7 1.0 convert_reduce_fusion
  1.7 1.0 fusion.7
  2.7 1.2 fusion.24
  4.0 2.4 %collective-permute-start = (bf16[48,256]{1,0:T(8,128)(2,1)S(1)}, bf16[48,256]{1,0:T(8,128)(2,1)S(1)}, u32[]{:S(2)}, u32[]{:S(2)}) collective-permute-start(bf16[48,256]{1,0:T(8,128)(2,1)S(1)} %get-tuple-element.34), channel_id=1, source_target_pairs={{0,1},{1,2},{2,3},{3,4},{4,5},{5,6},{6,7},{7,8},{8,9},{9,10},{10,1... | collective-permute-start | bytes 73736 | tf_op jit(solution)/shard_map/ppermute | solution.py:421
  6.3 1.3 collective-permute-start.1
  7.7 0.7 slice_bitcast_fusion
  8.4 0.7 bitcast_dynamic-update-slice_fusion.heads_ref
  9.1 0.8 dynamic-slice_subtract_fusion.1
  9.8 0.7 dynamic-slice_subtract_fusion
  10.5 0.9 slice_multiply_fusion
  11.4 0.0 copy-done.9
  11.4 0.1 fusion.20
  11.5 0.0 copy-done
  11.5 1.1 compare_convert_fusion.of_head
  12.7 0.0 copy-done.8
  12.7 0.0 copy-start.7
  12.7 3.4 %copy-done.7 = bf16[256,128,128]{2,1,0:T(8,128)(2,1)S(1)} copy-done((bf16[256,128,128]{2,1,0:T(8,128)(2,1)S(1)}, bf16[256,128,128]{2,1,0:T(8,128)(2,1)}, u32[]{:S(2)}) %copy-start.7) | copy-done | bytes 8388632
  16.1 0.0 copy-start.6
  16.1 0.0 copy-start.10
  16.1 0.0 copy-start.11
  16.1 39.2 %shard_map.176 = (bf16[4,256,128]{2,1,0:T(8,128)(2,1)S(1)}, bf16[16,256,128]{2,1,0:T(8,128)(2,1)S(1)}) custom-call(bf16[256,128,128]{2,1,0:T(8,128)(2,1)S(1)} %copy-done.7, bf16[128,512]{1,0:T(8,128)(2,1)S(1)} %pad_maximum_fusion.up_ref, bf16[256,128]{1,0:T(8,128)(2,1)S(1)} %copy-done.8, bf16[32,128]{1,0:T(8,128)(2,1)S(1)} %bitcast_dynamic-update-slice_fusion.heads_ref), custom_call_target="tpu_custom_call" | custom-call | flops 6610223104 | bytes 9699328 | tf_op jit(solution)/shard_map/pallas_call | solution.py:83
  55.3 0.0 copy-start.2
  55.3 1.0 copy-done.2
  56.3 0.0 copy-done.6
  56.3 0.0 copy-start.1
  56.3 0.0 copy-start.3
  56.3 0.0 copy-start.4
  56.3 0.0 copy-start.5
  56.3 0.1 dynamic-slice_bitcast_fusion
  56.4 0.0 copy-done.10
  56.4 0.1 copy.21.own_chain
  56.5 0.1 copy.20.query_tok
  56.7 0.0 copy-done.11
  56.7 0.1 broadcast_in_dim.33
  56.8 0.3 broadcast_in_dim_reshape.4.chain_rows
  57.0 0.0 collective-permute-done
  57.1 0.0 collective-permute-done.1
  57.1 0.0 copy-done.1
  57.1 0.1 copy-done.3
  57.2 0.1 copy-done.4
  57.3 0.0 copy-done.5
  57.3 85.4 %shard_map.177 = (bf16[8,32,768]{2,1,0:T(8,128)(2,1)}, bf16[256,128]{1,0:T(8,128)(2,1)S(1)}) custom-call(bf16[4,256,128]{2,1,0:T(8,128)(2,1)S(1)} %get-tuple-element.30.atom_bias, bf16[16,256,128]{2,1,0:T(8,128)(2,1)} %copy-done.2, bf16[768,3072]{1,0:T(8,128)(2,1)} %proj_hbm.1, bf16[768,768]{1,0:T(8,128)(2,1)} %exit_hbm.1, ...), custom_call_target="tpu_custom_call" | custom-call | tf_op jit(solution)/shard_map/pallas_call | solution.py:485
  142.7 1.8 %copy.26 = bf16[256,768]{1,0:T(8,128)(2,1)} copy(bf16[256,768]{1,0:T(8,128)(2,1)} %bitcast.13) | data formatting | bytes 786432
  144.5 0.6 copy.27
  (15 shorter events, 0.1 us)
Async XLA Ops:
  0.6 10.9 %copy-start = (bf16[256,768]{1,0:T(8,128)(2,1)S(1)}, bf16[256,768]{1,0:T(8,128)(2,1)}, u32[]{:S(2)}) copy-start(bf16[256,768]{1,0:T(8,128)(2,1)} %param.22) | copy-start | bytes 1179652
  0.6 10.8 %copy-start.9 = (s32[8192]{0:T(1024)S(1)}, s32[8192]{0:T(1024)}, u32[]{:S(2)}) copy-start(s32[8192]{0:T(1024)} %param.24) | copy-start | bytes 98308
  0.7 12.0 %copy-start.8 = (bf16[256,128]{1,0:T(8,128)(2,1)S(1)}, bf16[256,128]{1,0:T(8,128)(2,1)}, u32[]{:S(2)}) copy-start(bf16[256,128]{1,0:T(8,128)(2,1)} %down_ref.1) | copy-start | bytes 196612
  4.0 53.1 %collective-permute-start = (bf16[48,256]{1,0:T(8,128)(2,1)S(1)}, bf16[48,256]{1,0:T(8,128)(2,1)S(1)}, u32[]{:S(2)}, u32[]{:S(2)}) collective-permute-start(bf16[48,256]{1,0:T(8,128)(2,1)S(1)} %get-tuple-element.34), channel_id=1, source_target_pairs={{0,1},{1,2},{2,3},{3,4},{4,5},{5,6},{6,7},{7,8},{8,9},{9,10},{10,1... | collective-permute-start | bytes 73736 | tf_op jit(solution)/shard_map/ppermute | solution.py:421
  6.3 50.7 %collective-permute-start.1 = (bf16[48,256]{1,0:T(8,128)(2,1)S(1)}, bf16[48,256]{1,0:T(8,128)(2,1)S(1)}, u32[]{:S(2)}, u32[]{:S(2)}) collective-permute-start(bf16[48,256]{1,0:T(8,128)(2,1)S(1)} %get-tuple-element.35), channel_id=1, source_target_pairs={{1,0},{2,1},{3,2},{4,3},{5,4},{6,5},{7,6},{8,7},{9,8},{10,9},{11,1... | collective-permute-start | bytes 73736 | tf_op jit(solution)/shard_map/ppermute | solution.py:423
  12.7 3.4 %copy-start.7 = (bf16[256,128,128]{2,1,0:T(8,128)(2,1)S(1)}, bf16[256,128,128]{2,1,0:T(8,128)(2,1)}, u32[]{:S(2)}) copy-start(bf16[256,128,128]{2,1,0:T(8,128)(2,1)} %x_ref.1) | copy-start | bytes 25165828
  16.1 40.2 %copy-start.6 = (s32[1024]{0:T(1024)S(1)}, s32[1024]{0:T(1024)}, u32[]{:S(2)}) copy-start(s32[1024]{0:T(1024)} %param.25) | copy-start | bytes 12292
  16.1 40.4 %copy-start.10 = (f32[768]{0:T(1024)S(1)}, f32[768]{0:T(1024)}, u32[]{:S(2)}) copy-start(f32[768]{0:T(1024)} %param.33) | copy-start | bytes 9220
  16.1 40.6 %copy-start.11 = (f32[16]{0:T(128)S(1)}, f32[16]{0:T(128)}, u32[]{:S(2)}) copy-start(f32[16]{0:T(128)} %param.36) | copy-start | bytes 196
  55.3 1.0 copy-start.2
  56.3 0.8 copy-start.1
  56.3 1.0 copy-start.3
  56.3 1.1 copy-start.4
  56.3 1.1 copy-start.5

commit v3 on v2

--- a/solution.py
+++ b/solution.py
@@ -50,72 +50,223 @@
     return x.astype(F32) + dot(hidden, down)
 
 
-def pair_kernel(sub, x_ref, up_ref, down_ref, heads_ref, atom_ref, token_ref, stage):
-    rows, cols, _ = x_ref.shape
-    groups = rows // sub
-
-    def load(g):
-        return x_ref[g * sub : (g + 1) * sub].reshape(sub * cols, CZ)
-
-    mixed, updated = {}, {}
-    for step in range(groups + 2):
-        if step < groups:
-            mixed[step] = pair_up_part(load(step), up_ref[...])
-        g = step - 1
-        if 0 <= g < groups:
-            updated[g] = pair_down_part(load(g), mixed.pop(g), down_ref[...])
-        g = step - 2
-        if 0 <= g < groups:
-            found = dot_nt(heads_ref[...], standardize(updated.pop(g)).astype(BF16))
-            for i in range(sub):
-                stage[:, g * sub + i, :] = found[:, i * cols : (i + 1) * cols]
-    token_ref[...] = stage[:HT].astype(BF16)
-    atom_ref[...] = stage[HT : HT + HA].astype(BF16)
+FAR = 1 << 20
+MESH = pl.DeviceIdType.MESH
+VMEM_LIMIT = 58 * 1024 * 1024
+
+
+def send(src, dst, send_sem, recv_sem, row, col):
+    return pltpu.make_async_remote_copy(
+        src_ref=src,
+        dst_ref=dst,
+        send_sem=send_sem,
+        recv_sem=recv_sem,
+        device_id=(row, col),
+        device_id_type=MESH,
+    )
+
+
+def band_span(s, tok_rows, tok_cols, unit):
+    at = (s - 1) * tok_cols
+    reach = QB + EDGE - 1
+    low = max(0, at - reach) // unit * unit
+    high = min(tok_rows, -(-(at + tok_cols + reach) // unit) * unit)
+    return low, high
+
+
+def pair_kernel(
+    ncol,
+    sub,
+    pair,
+    up_ref,
+    down_ref,
+    heads_ref,
+    own_bias,
+    band,
+    cells,
+    up,
+    stage,
+    token_buf,
+    atom_buf,
+    cell_sem,
+    bias_send,
+    bias_recv,
+    band_send,
+    band_pass,
+    band_recv,
+    keep_sem,
+):
+    r, c = lax.axis_index("row"), lax.axis_index("col")
+    side = lax.rem(c, 2)
+    partner = c + 1 - 2 * side
+    half = ncol // 2
+    slots, _, tok_rows, tok_cols = band.shape
+    ratio = tok_rows // tok_cols
+    own = tok_rows // ncol
+    groups = own // sub
+
+    barrier = pltpu.get_barrier_semaphore()
+    for k in range(1, ncol):
+        pl.semaphore_signal(barrier, inc=1, device_id=(r, lax.rem(c + k, ncol)), device_id_type=MESH)
+
+    def fetch(i):
+        at = pl.multiple_of(lax.rem(c + 1 + i, ncol) * own, own)
+        slot = lax.rem(i, 2)
+        return pltpu.make_async_copy(pair.at[pl.ds(at, own)], cells.at[slot], cell_sem.at[slot])
+
+    fetch(0).start()
+    up[:, :PH] = (up_ref[:, :PH].astype(F32) * 0.5).astype(BF16)
+    up[:, PH:] = up_ref[:, PH:]
+    pl.semaphore_wait(barrier, ncol - 1)
+
+    def source(s):
+        col = r * ratio + s - 1
+        return col, (col >= 0) & (col < ncol)
+
+    def chunk(i):
+        peer = lax.rem(c + 1 + i, ncol)
+        return peer, pl.multiple_of(peer * own, own)
+
+    def own_copy(i):
+        return pltpu.make_async_copy(token_buf.at[i], own_bias.at[c], keep_sem.at[0])
+
+    def peer_copy(i):
+        peer, _ = chunk(i)
+        return send(token_buf.at[i], own_bias.at[c], bias_send.at[i], bias_recv.at[i], r, peer)
+
+    def one(i, _):
+        fetch(i).wait()
+
+        @pl.when(i + 1 < ncol)
+        def _():
+            fetch(i + 1).start()
+
+        slot = lax.rem(i, 2)
+        peer, at = chunk(i)
+
+        def load(g):
+            return cells[slot, g * sub : (g + 1) * sub].reshape(sub * tok_cols, CZ)
+
+        mixed, updated = {}, {}
+        for step in range(groups + 2):
+            if step < groups:
+                mixed[step] = pair_up_part(load(step), up[...])
+            g = step - 1
+            if 0 <= g < groups:
+                updated[g] = pair_down_part(load(g), mixed.pop(g), down_ref[...])
+            g = step - 2
+            if 0 <= g < groups:
+                found = dot_nt(heads_ref[...], standardize(updated.pop(g)).astype(BF16))
+                for n in range(sub):
+                    stage[:, g * sub + n, :] = found[:, n * tok_cols : (n + 1) * tok_cols]
+        token_buf[i] = stage[HA:HB].astype(BF16)
+        atom_buf[i] = stage[:HA].astype(BF16)
+
+        for s in range(slots):
+            low, high = band_span(s, tok_rows, tok_cols, own)
+            col, _ = source(s)
+
+            @pl.when((c == col) & (at >= low) & (at < high))
+            def _():
+                dst = band.at[s, :, pl.ds(at, own), :]
+                for k in range(half):
+                    to = partner if k == 0 else lax.rem(c + 2 * k, ncol)
+                    send(atom_buf.at[i], dst, band_send.at[k], band_recv.at[s], r, to).start()
+                pltpu.make_async_copy(atom_buf.at[i], dst, keep_sem.at[1]).start()
+
+        @pl.when(i + 1 < ncol)
+        def _():
+            peer_copy(i).start()
+
+        return 0
+
+    lax.fori_loop(0, ncol, one, 0)
+    own_copy(ncol - 1).start()
+
+    def block(s):
+        low, high = band_span(s, tok_rows, tok_cols, own)
+        return band.at[s, :, pl.ds(low, high - low), :]
+
+    def passed(s):
+        return send(block(s), block(s), band_pass.at[s], band_recv.at[s], r, partner)
+
+    for s in range(slots):
+        col, there = source(s)
+
+        @pl.when(there & (c != col) & (lax.rem(col + 2, 2) == side))
+        def _():
+            passed(s).wait_recv()
+            passed(s).start()
+
+    for s in range(slots):
+        col, there = source(s)
+
+        @pl.when(there & (lax.rem(col + 2, 2) != side))
+        def _():
+            passed(s).wait_recv()
+
+        @pl.when(c == col)
+        def _():
+            pltpu.make_async_copy(block(s), block(s), keep_sem.at[1]).wait()
+            for k in range(half):
+                send(block(s), block(s), band_send.at[k], band_recv.at[s], r, partner).wait_send()
+
+        @pl.when(there & (c != col) & (lax.rem(col + 2, 2) == side))
+        def _():
+            passed(s).wait_send()
+
+    own_copy(ncol - 1).wait()
+    for i in range(ncol - 1):
+        peer_copy(i).wait()
 
 
 def pair_bias(pair_tensor, pair_up, pair_down, bias_heads):
     tok_rows, tok_cols, _ = pair_tensor.shape
-    tile = 32
-    up = jnp.concatenate([pair_up[:, :PH] * 0.5, pair_up[:, PH:]], axis=1).astype(BF16)
-    heads = jnp.zeros((32, CZ), BF16)
-    heads = heads.at[:HT].set(bias_heads[:, HA:].T).at[HT : HT + HA].set(bias_heads[:, :HA].T)
+    ncol = lax.axis_size("col")
+    own = tok_rows // ncol
+    slots = tok_rows // tok_cols + 2
     pairs = tok_rows * tok_cols
+    dma = pltpu.SemaphoreType.DMA
+    vmem = pl.BlockSpec(memory_space=pltpu.VMEM)
+    anywhere = pl.BlockSpec(memory_space=pl.ANY)
     return pl.pallas_call(
-        functools.partial(pair_kernel, 2),
-        grid=(tok_rows // tile,),
-        in_specs=[
-            pl.BlockSpec((tile, tok_cols, CZ), lambda i: (i, 0, 0)),
-            pl.BlockSpec((CZ, 2 * PH), lambda i: (0, 0)),
-            pl.BlockSpec((PH, CZ), lambda i: (0, 0)),
-            pl.BlockSpec((32, CZ), lambda i: (0, 0)),
+        functools.partial(pair_kernel, ncol, 2),
+        in_specs=[anywhere, vmem, vmem, vmem],
+        out_specs=[anywhere, anywhere],
+        out_shape=[
+            jax.ShapeDtypeStruct((ncol, HT, own, tok_cols), BF16),
+            jax.ShapeDtypeStruct((slots, HA, tok_rows, tok_cols), BF16),
         ],
-        out_specs=[
-            pl.BlockSpec((HA, tile, tok_cols), lambda i: (0, i, 0)),
-            pl.BlockSpec((HT, tile, tok_cols), lambda i: (0, i, 0)),
+        scratch_shapes=[
+            pltpu.VMEM((2, own, tok_cols, CZ), BF16),
+            pltpu.VMEM((CZ, 2 * PH), BF16),
+            pltpu.VMEM((HB, own, tok_cols), F32),
+            pltpu.VMEM((ncol, HT, own, tok_cols), BF16),
+            pltpu.VMEM((ncol, HA, own, tok_cols), BF16),
+            dma((2,)),
+            dma((ncol,)),
+            dma((ncol,)),
+            dma((ncol // 2,)),
+            dma((slots,)),
+            dma((slots,)),
+            dma((2,)),
         ],
-        out_shape=[
-            jax.ShapeDtypeStruct((HA, tok_rows, tok_cols), BF16),
-            jax.ShapeDtypeStruct((HT, tok_rows, tok_cols), BF16),
-        ],
-        scratch_shapes=[pltpu.VMEM((32, tile, tok_cols), F32)],
-        compiler_params=pltpu.CompilerParams(vmem_limit_bytes=32 * 1024 * 1024),
+        compiler_params=pltpu.CompilerParams(
+            collective_id=0, has_side_effects=True, vmem_limit_bytes=VMEM_LIMIT
+        ),
         cost_estimate=pl.CostEstimate(
             flops=2 * pairs * (2 * CZ * PH + PH * CZ + CZ * HB),
             bytes_accessed=2 * pairs * (CZ + HB),
             transcendentals=pairs * PH,
         ),
-    )(pair_tensor, up, pair_down, heads)
-
-
-FAR = 1 << 20
-MESH = pl.DeviceIdType.MESH
+    )(pair_tensor, pair_up, pair_down, bias_heads.T)
 
 
 def after_kernel(
     nrow,
     ncol,
-    atom_bias,
-    token_bias,
+    bias_hbm,
+    band_hbm,
     proj_hbm,
     exit_hbm,
     queries,
@@ -129,7 +280,6 @@
     own_chain,
     all_chain,
     single,
-    of_head,
     atom_exit,
     atom_pool,
     token_gain,
@@ -145,10 +295,7 @@
     proj,
     exit_w,
     local_sem,
-    band_send,
-    band_pass,
-    band_recv,
-    bias_sem,
+    band_sem,
     mid_sem,
     tok_send,
     tok_recv,
@@ -167,117 +314,47 @@
     atom_rows = queries.shape[0]
     tokens = all_chain.shape[1]
 
-    def send(src, dst, send_sem, recv_sem, row, col):
-        return pltpu.make_async_remote_copy(
-            src_ref=src,
-            dst_ref=dst,
-            send_sem=send_sem,
-            recv_sem=recv_sem,
-            device_id=(row, col),
-            device_id_type=MESH,
-        )
-
     barrier = pltpu.get_barrier_semaphore()
-    for k in range(1, ncol):
-        pl.semaphore_signal(barrier, inc=1, device_id=(r, lax.rem(c + k, ncol)), device_id_type=MESH)
+    for k in range(1, half):
+        pl.semaphore_signal(barrier, inc=1, device_id=(r, lax.rem(c + 2 * k, ncol)), device_id_type=MESH)
+    pl.semaphore_signal(barrier, inc=1, device_id=(r, partner), device_id_type=MESH)
     for k in range(1, nrow):
         pl.semaphore_signal(barrier, inc=1, device_id=(lax.rem(r + k, nrow), c), device_id_type=MESH)
 
     loads = [
         pltpu.make_async_copy(proj_hbm, proj, local_sem.at[0]),
         pltpu.make_async_copy(exit_hbm, exit_w, local_sem.at[1]),
-        pltpu.make_async_copy(
-            token_bias.at[:, pl.ds(pl.multiple_of(c * own, own), own), :], own_bias.at[c], local_sem.at[2]
-        ),
+        pltpu.make_async_copy(bias_hbm, own_bias, local_sem.at[2]),
     ]
+    spans = [band_span(s, tok_rows, tok_cols, own) for s in range(slots)]
+
+    def fetched(s):
+        low, high = spans[s]
+        return pltpu.make_async_copy(
+            band_hbm.at[s, :, pl.ds(low, high - low), :], band.at[s, :, pl.ds(low, high - low), :], band_sem.at[s]
+        )
+
+    def there(s):
+        col = r * ratio + s - 1
+        return (col >= 0) & (col < ncol)
+
+    for s in range(slots):
+        pl.when(there(s))(fetched(s).start)
     for load in loads:
         load.start()
-
-    def span(s):
-        at = (s - 1) * tok_cols
-        reach = QB + EDGE - 1
-        low = max(0, at - reach) // 16 * 16
-        high = min(tok_rows, -(-(at + tok_cols + reach) // 16) * 16)
-        return low, high
-
-    def source(s):
-        col = r * ratio + s - 1
-        return col, (col >= 0) & (col < ncol)
-
     for s in range(slots):
-        low, high = span(s)
+        low, high = spans[s]
         if low > 0:
             band[s, :, 0:low, :] = jnp.zeros((HA, low, tok_cols), BF16)
         if high < tok_rows:
             band[s, :, high:tok_rows, :] = jnp.zeros((HA, tok_rows - high, tok_cols), BF16)
 
-    pl.semaphore_wait(barrier, ncol - 1 + nrow - 1)
-
-    def block(s):
-        low, high = span(s)
-        return band.at[s, :, pl.ds(low, high - low), :]
-
-    def from_source(s, k):
-        low, high = span(s)
-        col = partner if k == 0 else lax.rem(c + 2 * k, ncol)
-        return send(
-            atom_bias.at[:, pl.ds(low, high - low), :], block(s), band_send.at[k], band_recv.at[s], r, col
-        )
-
-    def passed(s):
-        return send(block(s), block(s), band_pass.at[s], band_recv.at[s], r, partner)
-
-    def kept(s):
-        low, high = span(s)
-        return pltpu.make_async_copy(atom_bias.at[:, pl.ds(low, high - low), :], block(s), local_sem.at[3])
+        @pl.when(jnp.logical_not(there(s)))
+        def _():
+            band[s, :, low:high, :] = jnp.zeros((HA, high - low, tok_cols), BF16)
 
     for s in range(slots):
-        col, there = source(s)
-
-        @pl.when(c == col)
-        def _():
-            for k in list(range(1, half)) + [0]:
-                from_source(s, k).start()
-            kept(s).start()
-
-        @pl.when(jnp.logical_not(there))
-        def _():
-            low, high = span(s)
-            band[s, :, low:high, :] = jnp.zeros((HA, high - low, tok_cols), BF16)
-
-    for s in range(slots):
-        col, there = source(s)
-
-        @pl.when(there & (c != col) & (lax.rem(col + 2, 2) == side))
-        def _():
-            passed(s).wait_recv()
-            passed(s).start()
-
-    for s in range(slots):
-        col, there = source(s)
-
-        @pl.when(there & (lax.rem(col + 2, 2) != side))
-        def _():
-            passed(s).wait_recv()
-
-        @pl.when(c == col)
-        def _():
-            kept(s).wait()
-
-    biases = []
-    for k in range(1, ncol):
-        col = lax.rem(c + k, ncol)
-        biases.append(
-            send(
-                token_bias.at[:, pl.ds(pl.multiple_of(col * own, own), own), :],
-                own_bias.at[c],
-                bias_sem.at[0, k],
-                bias_sem.at[1, k],
-                r,
-                col,
-            )
-        )
-        biases[-1].start()
+        pl.when(there(s))(fetched(s).wait)
 
     padded = keys.shape[0]
     q_iota = lax.broadcasted_iota(jnp.int32, (atom_rows, padded), 0)
@@ -318,6 +395,7 @@
         for copy in over:
             copy.wait_recv()
 
+    pl.semaphore_wait(barrier, half + nrow - 1)
     out, over = gather_start(mids, mid_sem)
     sent = out + over
     gather_end(mids, mid_sem, out, over)
@@ -367,17 +445,18 @@
             over_to(k, j).wait_recv()
 
     keyval = dot(every[...].reshape(tokens, CS), proj[:, 2 * CS :]).astype(BF16)
-    spread = jnp.concatenate([query] * HT, axis=0) * of_head[...]
+    head_at = lax.broadcasted_iota(jnp.int32, (HT, own, CS), 0) * HDT
+    head_lane = lax.broadcasted_iota(jnp.int32, (HT, own, CS), 2)
+    of_head = ((head_lane >= head_at) & (head_lane < head_at + HDT)).astype(F32).reshape(HT * own, CS)
+    spread = jnp.concatenate([query] * HT, axis=0) * of_head.astype(BF16)
     same = (own_chain[...] == all_chain[...]).astype(F32)
     same = jnp.concatenate([same] * HT, axis=0) * chain_rows[...]
     loads[2].wait()
-    for copy in biases:
-        copy.wait_recv()
     bias = jnp.concatenate([own_bias[k].reshape(HT * own, tok_cols) for k in range(ncol)], axis=1)
     scores = dot_nt(spread, keyval[:, :CS]) * HDT ** (-0.5) + bias.astype(F32) + same
     weights = jnp.exp(scores - jnp.max(scores, axis=-1, keepdims=True))
     total = jnp.sum(weights, axis=-1, keepdims=True)
-    mixed = dot(weights.astype(BF16), keyval[:, CS:]) / total * of_head[...].astype(F32)
+    mixed = dot(weights.astype(BF16), keyval[:, CS:]) / total * of_head
     token_attended = jnp.sum(mixed.reshape(HT, own, CS), axis=0)
     token_gated = (token_attended * jax.nn.sigmoid(token_gate)).astype(BF16)
     loads[1].wait()
@@ -390,7 +469,7 @@
     token_sent = dot(updates[...].reshape(tok_rows, CS), token_back[...]).astype(BF16)
     atom_out[...] = (atom_mid.astype(F32) + dot(q_hot, token_sent)).astype(BF16)
 
-    for copy in sent + biases:
+    for copy in sent:
         copy.wait_send()
     for k in range(half):
         if k > 0:
@@ -399,17 +478,6 @@
             across(k, j).wait_send()
         for j in range(nrow):
             over_to(k, j).wait_send()
-    for s in range(slots):
-        col, there = source(s)
-
-        @pl.when(c == col)
-        def _():
-            for k in range(half):
-                from_source(s, k).wait_send()
-
-        @pl.when(there & (c != col) & (lax.rem(col + 2, 2) == side))
-        def _():
-            passed(s).wait_send()
 
 
 def with_halo(cells, axes, width):
@@ -463,7 +531,7 @@
     atom_gate = projected[:, 3 * CA :]
     extended = with_halo(keyvals, ("row", "col"), EDGE)
 
-    atom_bias, token_bias = pair_bias(pair_tensor, pair_up, pair_down, bias_heads)
+    bias, band = pair_bias(pair_tensor, pair_up, pair_down, bias_heads)
 
     reach = atom_rows + 2 * EDGE
     padded = -(-reach // 128) * 128
@@ -475,7 +543,6 @@
     row_tok = lax.dynamic_slice_in_dim(atom_token, row_index * row_atoms, row_atoms) - own_start
     own_chain = lax.dynamic_slice_in_dim(chain_index, own_start, own)
     single = lax.dynamic_slice_in_dim(token_single, col_index * own, own)
-    of_head = jnp.arange(CS)[None, :] // HDT == jnp.arange(HT * own)[:, None] // own
     row_count = lax.axis_size("row")
     slots = tok_rows // tok_cols + 2
     half = col_count // 2
@@ -484,7 +551,7 @@
     dma = pltpu.SemaphoreType.DMA
     token_update, atom_update = pl.pallas_call(
         functools.partial(after_kernel, row_count, col_count),
-        in_specs=[anywhere] * 4 + [vmem] * 17,
+        in_specs=[anywhere] * 4 + [vmem] * 16,
         out_specs=[vmem, vmem],
         out_shape=[
             jax.ShapeDtypeStruct((col_count, own, CS), BF16),
@@ -499,10 +566,7 @@
             pltpu.VMEM(token_proj.shape, BF16),
             pltpu.VMEM(token_exit.shape, BF16),
             dma((4,)),
-            dma((half,)),
             dma((slots,)),
-            dma((slots,)),
-            dma((2, col_count)),
             dma((4, half)),
             dma((half, row_count)),
             dma((half, row_count)),
@@ -511,11 +575,11 @@
             dma((4, half)),
         ],
         compiler_params=pltpu.CompilerParams(
-            collective_id=0, has_side_effects=True, vmem_limit_bytes=52 * 1024 * 1024
+            collective_id=1, has_side_effects=True, vmem_limit_bytes=VMEM_LIMIT
         ),
     )(
-        atom_bias,
-        token_bias,
+        bias,
+        band,
         token_proj,
         token_exit,
         queries,
@@ -529,7 +593,6 @@
         own_chain[:, None],
         chain_index[None, :],
         single,
-        of_head.astype(BF16),
         atom_exit,
         atom_pool,
         token_gain[None, :],

time: 146 us -> 122 us (0.84)
  Pallas kernels: 125 us -> 100 us
    pallas_call x1, Pallas kernels: 85.4 us -> 49 us  [local(): pl.pallas_call(functools.partial(after_kernel, row_count, col_count), in_...]
    pallas_call x1, Pallas kernels: 39.2 us -> 51.2 us  [pair_bias(): pl.pallas_call(functools.partial(pair_kernel, ncol, 2), in_specs=[anywher...]
    unnamed x26 -> x8, local copies, waits for them, and re-layouts: 7.01 us -> 3.26 us
  transfers between devices with their start and end apart: 2 -> 2, of which waited for: 0 -> 0; matrix products, arithmetic and copies ran while one was open for 4% -> 8% of each run, Pallas kernels for 27% -> 42%
where the time goes in v3:
time: 122 us; the launch traced here: 121 us
  Pallas kernels  100 us (82%)
  local copies, waits for them, and re-layouts  10.4 us (9%)
  other arithmetic  4.87 us (4%)
  starting transfers between devices  3.65 us (3%)
  matrix products  1.24 us (1%)
    pallas_call x1, Pallas kernels, pair_bias(): pl.pallas_call(functools.partial(pair_kernel, ncol, 2), in_specs=[anywher...  51.2 us
    pallas_call x1, Pallas kernels, local(): pl.pallas_call(functools.partial(after_kernel, row_count, col_count), in_...  49 us
    unnamed x8, local copies, waits for them, and re-layouts  3.26 us
  transfers between devices with their start and end apart: 2, of which 0 were waited for; matrix products, arithmetic and copies ran while one was open for 8% of the time, Pallas kernels for 42%

profile of v3, /device:TPU:0, one launch (start us, length us, event | category | flops | bytes accessed | tf_op | source)
XLA Modules:
  0.0 121.0 jit_solution(7775039055379654791)
XLA Ops:
  0.6 0.0 copy-start
  0.6 1.0 convert_reduce_fusion
  1.7 1.0 fusion.7
  2.7 1.2 %fusion.18 = (bf16[256,512]{1,0:T(8,128)(2,1)S(1)}, f32[256,512]{1,0:T(8,128)S(1)}) fusion(bf16[128,512]{1,0:T(8,128)(2,1)} %param.26, bf16[256,128]{1,0:T(8,128)(2,1)} %atom_single.1, f32[128]{0:T(128)} %param.25, f32[256]{0:T(256)S(1)} %add_rsqrt_fusion, f32[256]{0:T(256)S(1)} %broadcast_multiply_fusion), kind=kOutput, calls=%fused_computation.27 | convolution fusion | flops 33849344 | bytes 985600 | tf_op jit(solution)/shard_map/dot_general | solution.py:36
  3.9 2.4 %collective-permute-start = (bf16[48,256]{1,0:T(8,128)(2,1)S(1)}, bf16[48,256]{1,0:T(8,128)(2,1)S(1)}, u32[]{:S(2)}, u32[]{:S(2)}) collective-permute-start(bf16[48,256]{1,0:T(8,128)(2,1)S(1)} %get-tuple-element.10), channel_id=1, source_target_pairs={{0,1},{1,2},{2,3},{3,4},{4,5},{5,6},{6,7},{7,8},{8,9},{9,10},{10,1... | collective-permute-start | bytes 73736 | tf_op jit(solution)/shard_map/ppermute | solution.py:489
  6.3 1.3 %collective-permute-start.1 = (bf16[48,256]{1,0:T(8,128)(2,1)S(1)}, bf16[48,256]{1,0:T(8,128)(2,1)S(1)}, u32[]{:S(2)}, u32[]{:S(2)}) collective-permute-start(bf16[48,256]{1,0:T(8,128)(2,1)S(1)} %get-tuple-element.11), channel_id=1, source_target_pairs={{1,0},{2,1},{3,2},{4,3},{5,4},{6,5},{7,6},{8,7},{9,8},{10,9},{11,1... | collective-permute-start | bytes 73736 | tf_op jit(solution)/shard_map/ppermute | solution.py:491
  7.6 0.8 dynamic-slice_subtract_fusion.1
  8.4 1.3 %dynamic-slice_subtract_fusion = s32[2048]{0:T(1024)} fusion(s32[8192]{0:T(1024)} %param.20, s32[]{:T(128)S(6)} %select_n.17, s32[]{:T(128)S(6)} %add.43), kind=kLoop, calls=%fused_computation.18 | loop fusion | flops 2048 | bytes 16392 | tf_op jit(solution)/shard_map/sub | solution.py:543
  9.7 0.8 fusion.15
  10.5 0.0 copy-done
  10.5 0.6 constant_dynamic-slice_fusion.single
  11.1 0.0 copy-start.1
  11.1 0.0 copy-start.2
  11.1 51.2 %shard_map.176 = (bf16[8,16,32,128]{3,2,1,0:T(8,128)(2,1)}, bf16[4,4,256,128]{3,2,1,0:T(8,128)(2,1)}) custom-call(bf16[256,128,128]{2,1,0:T(8,128)(2,1)} %pair.1, bf16[128,512]{1,0:T(8,128)(2,1)} %up_ref.1, bf16[256,128]{1,0:T(8,128)(2,1)} %down_ref.1, bf16[20,128]{1,0:T(8,128)(2,1)} %bitcast.12), custom_call_target="tpu_custom_call" | custom-call | flops 6610223104 | bytes 9699328 | tf_op jit(solution)/shard_map/pallas_call | solution.py:232
  62.3 0.8 dynamic-slice_bitcast_fusion
  63.0 0.6 slice.32.queries
  63.7 0.6 broadcast_in_dim.25.key_tok
  64.3 0.0 copy-done.1
  64.3 0.6 broadcast_in_dim.29.token_gain
  64.9 0.7 copy.21.own_chain
  65.6 0.8 copy.20.query_tok
  66.4 0.0 copy-done.2
  66.4 0.1 broadcast_in_dim.30
  66.4 1.0 broadcast_in_dim_reshape.4.chain_rows
  67.4 0.7 slice.33.atom_gate
  68.1 0.0 collective-permute-done
  68.1 0.0 collective-permute-done.1
  68.1 0.7 fusion.17
  68.8 49.0 %shard_map.177 = (bf16[8,32,768]{2,1,0:T(8,128)(2,1)}, bf16[256,128]{1,0:T(8,128)(2,1)}) custom-call(bf16[8,16,32,128]{3,2,1,0:T(8,128)(2,1)} %get-tuple-element.6.bias_hbm, bf16[4,4,256,128]{3,2,1,0:T(8,128)(2,1)} %get-tuple-element.7.band_hbm, bf16[768,3072]{1,0:T(8,128)(2,1)} %proj_hbm.1, bf16[768,768]{1,0:T(8,128)(2,1)} %exit_hbm.1, ...), custom_call_target="tpu_custom_call" | custom-call | tf_op jit(solution)/shard_map/pallas_call | solution.py:552
  117.8 1.8 %copy.25 = bf16[256,768]{1,0:T(8,128)(2,1)} copy(bf16[256,768]{1,0:T(8,128)(2,1)} %bitcast.8) | data formatting | bytes 786432
  119.5 1.5 %copy.26 = bf16[256,128]{1,0:T(8,128)(2,1)} copy(bf16[256,128]{1,0:T(8,128)(2,1)} %get-tuple-element.19) | data formatting | bytes 131072
  (5 shorter events, 0.0 us)
Async XLA Ops:
  0.6 9.8 %copy-start = (bf16[256,768]{1,0:T(8,128)(2,1)S(1)}, bf16[256,768]{1,0:T(8,128)(2,1)}, u32[]{:S(2)}) copy-start(bf16[256,768]{1,0:T(8,128)(2,1)} %param.18) | copy-start | bytes 1179652
  3.9 64.1 %collective-permute-start = (bf16[48,256]{1,0:T(8,128)(2,1)S(1)}, bf16[48,256]{1,0:T(8,128)(2,1)S(1)}, u32[]{:S(2)}, u32[]{:S(2)}) collective-permute-start(bf16[48,256]{1,0:T(8,128)(2,1)S(1)} %get-tuple-element.10), channel_id=1, source_target_pairs={{0,1},{1,2},{2,3},{3,4},{4,5},{5,6},{6,7},{7,8},{8,9},{9,10},{10,1... | collective-permute-start | bytes 73736 | tf_op jit(solution)/shard_map/ppermute | solution.py:489
  6.3 61.8 %collective-permute-start.1 = (bf16[48,256]{1,0:T(8,128)(2,1)S(1)}, bf16[48,256]{1,0:T(8,128)(2,1)S(1)}, u32[]{:S(2)}, u32[]{:S(2)}) collective-permute-start(bf16[48,256]{1,0:T(8,128)(2,1)S(1)} %get-tuple-element.11), channel_id=1, source_target_pairs={{1,0},{2,1},{3,2},{4,3},{5,4},{6,5},{7,6},{8,7},{9,8},{10,9},{11,1... | collective-permute-start | bytes 73736 | tf_op jit(solution)/shard_map/ppermute | solution.py:491
  11.1 53.2 %copy-start.1 = (f32[768]{0:T(1024)S(1)}, f32[768]{0:T(1024)}, u32[]{:S(2)}) copy-start(f32[768]{0:T(1024)} %param.29) | copy-start | bytes 9220
  11.1 55.3 %copy-start.2 = (f32[16]{0:T(128)S(1)}, f32[16]{0:T(128)}, u32[]{:S(2)}) copy-start(f32[16]{0:T(128)} %param.32) | copy-start | bytes 196

commit v4 on v3

--- a/solution.py
+++ b/solution.py
@@ -269,10 +269,8 @@
     band_hbm,
     proj_hbm,
     exit_hbm,
-    queries,
-    atom_gate,
-    keys,
-    vals,
+    projected,
+    grown,
     atom_single,
     query_tok,
     key_tok,
@@ -311,7 +309,7 @@
     slots = band.shape[0]
     ratio = tok_rows // tok_cols
     own = single.shape[0]
-    atom_rows = queries.shape[0]
+    atom_rows = atom_single.shape[0]
     tokens = all_chain.shape[1]
 
     barrier = pltpu.get_barrier_semaphore()
@@ -356,7 +354,7 @@
     for s in range(slots):
         pl.when(there(s))(fetched(s).wait)
 
-    padded = keys.shape[0]
+    padded = grown.shape[0]
     q_iota = lax.broadcasted_iota(jnp.int32, (atom_rows, padded), 0)
     k_iota = lax.broadcasted_iota(jnp.int32, (atom_rows, padded), 1) - EDGE
     first = jnp.bitwise_and(q_iota, -QB) - EDGE
@@ -369,13 +367,13 @@
         mine = ((lane >= h * HDA) & (lane < (h + 1) * HDA)).astype(F32)
         wide = jnp.concatenate([band[s, h] for s in range(slots)], axis=1)
         tile = dot(dot(q_hot, wide).astype(BF16), k_hot)
-        query = (queries[...].astype(F32) * mine).astype(BF16)
-        scores = dot_nt(query, keys[...]) * HDA ** (-0.5) + tile
+        query = (projected[:, :CA] * mine).astype(BF16)
+        scores = dot_nt(query, grown[:, :CA]) * HDA ** (-0.5) + tile
         scores = jnp.where(valid, scores, -1e30)
         weights = jnp.exp(scores - jnp.max(scores, axis=-1, keepdims=True))
         total = jnp.sum(weights, axis=-1, keepdims=True)
-        attended += dot(weights.astype(BF16), vals[...]) / total * mine
-    atom_gated = (attended * jax.nn.sigmoid(atom_gate[...])).astype(BF16)
+        attended += dot(weights.astype(BF16), grown[:, CA:]) / total * mine
+    atom_gated = (attended * jax.nn.sigmoid(projected[:, 3 * CA :])).astype(BF16)
     atom_mid = (atom_single[...].astype(F32) + dot(atom_gated, atom_exit[...])).astype(BF16)
     mids[c] = atom_mid
 
@@ -526,9 +524,7 @@
 
     atom_normed = (standardize(atom_single) * atom_gain).astype(BF16)
     projected = dot(atom_normed, atom_proj)
-    queries = projected[:, :CA].astype(BF16)
     keyvals = projected[:, CA : 3 * CA].astype(BF16)
-    atom_gate = projected[:, 3 * CA :]
     extended = with_halo(keyvals, ("row", "col"), EDGE)
 
     bias, band = pair_bias(pair_tensor, pair_up, pair_down, bias_heads)
@@ -551,7 +547,7 @@
     dma = pltpu.SemaphoreType.DMA
     token_update, atom_update = pl.pallas_call(
         functools.partial(after_kernel, row_count, col_count),
-        in_specs=[anywhere] * 4 + [vmem] * 16,
+        in_specs=[anywhere] * 4 + [vmem] * 14,
         out_specs=[vmem, vmem],
         out_shape=[
             jax.ShapeDtypeStruct((col_count, own, CS), BF16),
@@ -582,10 +578,8 @@
         band,
         token_proj,
         token_exit,
-        queries,
-        atom_gate,
-        grown[:, :CA],
-        grown[:, CA:],
+        projected,
+        grown,
         atom_single,
         query_tok[:, None],
         key_tok[None, :],

time: 122 us -> 121 us (level)
  local copies, waits for them, and re-layouts: 10.4 us -> 8.33 us
    slice x3 -> x0, local copies, waits for them, and re-layouts: 2 us -> none  [the longest x1 0.7 us: local(): grown[:, CA:]]
  transfers between devices with their start and end apart: 2 -> 2, of which waited for: 0 -> 0; matrix products, arithmetic and copies ran while one was open for 8% -> 7% of each run, Pallas kernels for 42% -> 42%
where the time goes in v4:
time: 121 us
  Pallas kernels  100 us (83%)
  local copies, waits for them, and re-layouts  8.33 us (7%)
  other arithmetic  5.56 us (5%)
  starting transfers between devices  3.64 us (3%)
  matrix products  2.04 us (2%)
    pallas_call x1, Pallas kernels, pair_bias(): pl.pallas_call(functools.partial(pair_kernel, ncol, 2), in_specs=[anywher...  51.2 us
    pallas_call x1, Pallas kernels, local(): pl.pallas_call(functools.partial(after_kernel, row_count, col_count), in_...  49.1 us
    unnamed x8, local copies, waits for them, and re-layouts  3.26 us
  transfers between devices with their start and end apart: 2, of which 0 were waited for; matrix products, arithmetic and copies ran while one was open for 7% of the time, Pallas kernels for 42%

profile of v4, /device:TPU:0, one launch (start us, length us, event | category | flops | bytes accessed | tf_op | source)
XLA Modules:
  0.0 120.5 jit_solution(15320079110506015409)
XLA Ops:
  0.6 0.0 copy-start
  0.6 1.0 convert_reduce_fusion
  1.7 1.0 fusion.7
  2.7 2.0 %fusion.17 = (bf16[256,512]{1,0:T(8,128)(2,1)S(1)}, f32[256,512]{1,0:T(8,128)}) fusion(bf16[128,512]{1,0:T(8,128)(2,1)} %param.26, bf16[256,128]{1,0:T(8,128)(2,1)} %atom_single.1, f32[128]{0:T(128)} %param.25, f32[256]{0:T(256)S(1)} %add_rsqrt_fusion, f32[256]{0:T(256)S(1)} %broadcast_multiply_fusion), kind=kOutput, calls=%fused_computation.26 | convolution fusion | flops 33849344 | bytes 985600 | tf_op jit(solution)/shard_map/dot_general | solution.py:36
  4.7 2.3 %collective-permute-start = (bf16[48,256]{1,0:T(8,128)(2,1)S(1)}, bf16[48,256]{1,0:T(8,128)(2,1)S(1)}, u32[]{:S(2)}, u32[]{:S(2)}) collective-permute-start(bf16[48,256]{1,0:T(8,128)(2,1)S(1)} %get-tuple-element.10), channel_id=1, source_target_pairs={{0,1},{1,2},{2,3},{3,4},{4,5},{5,6},{6,7},{7,8},{8,9},{9,10},{10,1... | collective-permute-start | bytes 73736 | tf_op jit(solution)/shard_map/ppermute | solution.py:487
  7.1 1.3 %collective-permute-start.1 = (bf16[48,256]{1,0:T(8,128)(2,1)S(1)}, bf16[48,256]{1,0:T(8,128)(2,1)S(1)}, u32[]{:S(2)}, u32[]{:S(2)}) collective-permute-start(bf16[48,256]{1,0:T(8,128)(2,1)S(1)} %get-tuple-element.11), channel_id=1, source_target_pairs={{1,0},{2,1},{3,2},{4,3},{5,4},{6,5},{7,6},{8,7},{9,8},{10,9},{11,1... | collective-permute-start | bytes 73736 | tf_op jit(solution)/shard_map/ppermute | solution.py:489
  8.4 0.8 dynamic-slice_subtract_fusion.1
  9.2 1.3 %dynamic-slice_subtract_fusion = s32[2048]{0:T(1024)} fusion(s32[8192]{0:T(1024)} %param.20, s32[]{:T(128)S(6)} %select_n.17, s32[]{:T(128)S(6)} %add.43), kind=kLoop, calls=%fused_computation.18 | loop fusion | flops 2048 | bytes 16392 | tf_op jit(solution)/shard_map/sub | solution.py:539
  10.5 0.8 fusion.15
  11.2 0.0 copy-done
  11.2 0.6 constant_dynamic-slice_fusion.single
  11.9 0.0 copy-start.1
  11.9 0.0 copy-start.2
  11.9 51.2 %shard_map.176 = (bf16[8,16,32,128]{3,2,1,0:T(8,128)(2,1)}, bf16[4,4,256,128]{3,2,1,0:T(8,128)(2,1)}) custom-call(bf16[256,128,128]{2,1,0:T(8,128)(2,1)} %pair.1, bf16[128,512]{1,0:T(8,128)(2,1)} %up_ref.1, bf16[256,128]{1,0:T(8,128)(2,1)} %down_ref.1, bf16[20,128]{1,0:T(8,128)(2,1)} %bitcast.12), custom_call_target="tpu_custom_call" | custom-call | flops 6610223104 | bytes 9699328 | tf_op jit(solution)/shard_map/pallas_call | solution.py:232
  63.0 0.8 dynamic-slice_bitcast_fusion
  63.8 0.6 broadcast_in_dim.25.key_tok
  64.4 0.0 copy-done.1
  64.4 0.6 broadcast_in_dim.29.token_gain
  65.0 0.7 copy.21.own_chain
  65.7 0.8 copy.20.query_tok
  66.5 0.0 copy-done.2
  66.5 0.1 broadcast_in_dim.30
  66.5 1.0 broadcast_in_dim_reshape.4.chain_rows
  67.5 0.0 collective-permute-done
  67.5 0.0 collective-permute-done.1
  67.5 0.7 fusion.4.grown
  68.2 49.1 %shard_map.177 = (bf16[8,32,768]{2,1,0:T(8,128)(2,1)}, bf16[256,128]{1,0:T(8,128)(2,1)}) custom-call(bf16[8,16,32,128]{3,2,1,0:T(8,128)(2,1)} %get-tuple-element.6.bias_hbm, bf16[4,4,256,128]{3,2,1,0:T(8,128)(2,1)} %get-tuple-element.7.band_hbm, bf16[768,3072]{1,0:T(8,128)(2,1)} %proj_hbm.1, bf16[768,768]{1,0:T(8,128)(2,1)} %exit_hbm.1, ...), custom_call_target="tpu_custom_call" | custom-call | tf_op jit(solution)/shard_map/pallas_call | solution.py:548
  117.3 1.8 %copy.25 = bf16[256,768]{1,0:T(8,128)(2,1)} copy(bf16[256,768]{1,0:T(8,128)(2,1)} %bitcast.8) | data formatting | bytes 786432
  119.1 1.5 %copy.26 = bf16[256,128]{1,0:T(8,128)(2,1)} copy(bf16[256,128]{1,0:T(8,128)(2,1)} %get-tuple-element.17) | data formatting | bytes 131072
  (4 shorter events, 0.0 us)
Async XLA Ops:
  0.6 10.6 %copy-start = (bf16[256,768]{1,0:T(8,128)(2,1)S(1)}, bf16[256,768]{1,0:T(8,128)(2,1)}, u32[]{:S(2)}) copy-start(bf16[256,768]{1,0:T(8,128)(2,1)} %param.18) | copy-start | bytes 1179652
  4.7 62.8 %collective-permute-start = (bf16[48,256]{1,0:T(8,128)(2,1)S(1)}, bf16[48,256]{1,0:T(8,128)(2,1)S(1)}, u32[]{:S(2)}, u32[]{:S(2)}) collective-permute-start(bf16[48,256]{1,0:T(8,128)(2,1)S(1)} %get-tuple-element.10), channel_id=1, source_target_pairs={{0,1},{1,2},{2,3},{3,4},{4,5},{5,6},{6,7},{7,8},{8,9},{9,10},{10,1... | collective-permute-start | bytes 73736 | tf_op jit(solution)/shard_map/ppermute | solution.py:487
  7.1 60.4 %collective-permute-start.1 = (bf16[48,256]{1,0:T(8,128)(2,1)S(1)}, bf16[48,256]{1,0:T(8,128)(2,1)S(1)}, u32[]{:S(2)}, u32[]{:S(2)}) collective-permute-start(bf16[48,256]{1,0:T(8,128)(2,1)S(1)} %get-tuple-element.11), channel_id=1, source_target_pairs={{1,0},{2,1},{3,2},{4,3},{5,4},{6,5},{7,6},{8,7},{9,8},{10,9},{11,1... | collective-permute-start | bytes 73736 | tf_op jit(solution)/shard_map/ppermute | solution.py:489
  11.9 52.5 %copy-start.1 = (f32[768]{0:T(1024)S(1)}, f32[768]{0:T(1024)}, u32[]{:S(2)}) copy-start(f32[768]{0:T(1024)} %param.29) | copy-start | bytes 9220
  11.9 54.6 %copy-start.2 = (f32[16]{0:T(128)S(1)}, f32[16]{0:T(128)}, u32[]{:S(2)}) copy-start(f32[16]{0:T(128)} %param.32) | copy-start | bytes 196
